TPU v7x, 256 devices: a whole 4x4x8 slice. The times are simulated.
256 devices in a mesh: dp: 64 (over z, x, core), head: 4 (over y).
Axes of the slice: x: 4, y: 4, z: 8, core: 2. Of those that a mesh axis runs over, the one named last changes fastest.
Arguments:
- q_raw: bfloat16 [98304, 2560], P('dp', 'head'), may hold values from -2000 to 2000
- k_raw: bfloat16 [98304, 512], P('dp', 'head'), may hold values from -2000 to 2000
- v_proj: bfloat16 [98304, 512], P('dp', 'head'), may hold values from -6 to 6
- d_out: bfloat16 [98304, 2560], P('dp', 'head'), may hold values from -6 to 6
- q_gain: float32 [2560], P('head'), may hold values from 0.5 to 2
- k_gain: float32 [512], P('head'), may hold values from 0.5 to 2
- doc_lengths: int32 [64, 36], P('dp'), may hold values from 1 to 381, as said below
- plan_dest: int32 [64, 36], P('dp'), may hold values from 0 to 63, as said below
- plan_offset: int32 [64, 36], P('dp'), may hold values from 0 to 24, as said below
Outputs:
- grad_q: bfloat16 [98304, 2560], P('dp', 'head')
- grad_k: bfloat16 [98304, 512], P('dp', 'head')
- grad_v: bfloat16 [98304, 512], P('dp', 'head')
- balanced_lse: float32 [20, 221184], P('head', 'dp')
Inputs may be any that keep to these rules, and one draw needn't show every extreme that they name: `doc_lengths`: each row holds the lengths of one sequence's documents in order and sums to 1536; the largest and the smallest length are reached in every draw. In each row exactly 32 documents have a plan_dest other than the row's own device, no two of them the same device; each of them has 24 to 48 rows, and in every row one has exactly 48 rows and one exactly 24. The documents that keep the row's own device sum to exactly 384 tokens. For a document sent to another device, plan_offset plus its length is at most 48; documents that stay have 0. Every row reaches the largest value.
All inputs are finite; a program needn't handle non-finite values.
Results may differ from a plain program's by a relative error of at most 0.008.
The roundings to bfloat16 on the way count: a program that leaves them out, or rounds other values in their place, can miss the bound.
Values may be sent and summed in bfloat16 or wider, within the bound.
No kernel may reach another device: no remote copies, remote signals or barrier semaphores. Data moves between devices by JAX's collectives and lax.ppermute only.
A program may use at most 128 MiB of HBM per device.

v0:
```python
import math

import jax
import jax.numpy as jnp
from jax import lax
from jax.sharding import PartitionSpec as P

HDIM = 128


eps = 1e-06
big_negative = -1e30


def block_backward(q_rows, k_rows, v_rows, grad_rows, tag_q, tag_k, pos_q, pos_k, head_dim):
    rows_q = q_rows.shape[0]
    rows_k = k_rows.shape[0]
    kv_local = k_rows.shape[1] // head_dim
    group_size = q_rows.shape[1] // k_rows.shape[1]
    queries = q_rows.reshape(rows_q, kv_local, group_size, head_dim)
    upstream = grad_rows.reshape(rows_q, kv_local, group_size, head_dim)
    key_heads = k_rows.reshape(rows_k, kv_local, head_dim)
    value_heads = v_rows.reshape(rows_k, kv_local, head_dim)
    scaling = 1.0 / math.sqrt(head_dim)
    allowed = (
        (tag_q[:, None] == tag_k[None, :])
        & (tag_q[:, None] >= 0)
        & (pos_k[None, :] <= pos_q[:, None])
    )
    scores = (
        jnp.einsum("qgjd,kgd->gjqk", queries, key_heads, preferred_element_type=jnp.float32)
        * scaling
    )
    masked = jnp.where(allowed, scores, big_negative)
    row_peak = jnp.max(masked, axis=-1, keepdims=True)
    row_total = jnp.sum(jnp.where(allowed, jnp.exp(masked - row_peak), 0.0), axis=-1, keepdims=True)
    row_live = row_total > 0.0
    log_sums = row_peak + jnp.log(jnp.where(row_live, row_total, 1.0))
    weights = jnp.where(allowed, jnp.exp(masked - log_sums), 0.0)
    weights_low = weights.astype(jnp.bfloat16)
    output = jnp.einsum(
        "gjqk,kgd->qgjd", weights_low, value_heads, preferred_element_type=jnp.float32
    )
    row_delta = jnp.transpose(jnp.sum(upstream.astype(jnp.float32) * output, axis=-1), (1, 2, 0))[
        ..., None
    ]
    grad_values = jnp.einsum(
        "gjqk,qgjd->kgd", weights_low, upstream, preferred_element_type=jnp.float32
    )
    grad_weights = jnp.einsum(
        "qgjd,kgd->gjqk", upstream, value_heads, preferred_element_type=jnp.float32
    )
    grad_low = (weights * (grad_weights - row_delta) * scaling).astype(jnp.bfloat16)
    grad_query = jnp.einsum(
        "gjqk,kgd->qgjd", grad_low, key_heads, preferred_element_type=jnp.float32
    )
    grad_keys = jnp.einsum("gjqk,qgjd->kgd", grad_low, queries, preferred_element_type=jnp.float32)
    log_rows = jnp.where(row_live[..., 0], log_sums[..., 0], 0.0).reshape(
        kv_local * group_size, rows_q
    )
    return (
        grad_query.reshape(rows_q, -1),
        grad_keys.reshape(rows_k, -1),
        grad_values.reshape(rows_k, -1),
        log_rows,
    )


def local(q_raw, k_raw, v_proj, d_out, q_gain, k_gain, doc_lengths, plan_dest, plan_offset):
    head_dim = HDIM
    seq_len = q_raw.shape[0]
    devices = lax.axis_size("dp")
    span = 2 * seq_len
    slot = span // devices
    home_count = seq_len // 4
    width_q = q_raw.shape[1] * lax.axis_size("head")
    width_k = k_raw.shape[1] * lax.axis_size("head")
    q_float = q_raw.astype(jnp.float32)
    k_float = k_raw.astype(jnp.float32)
    sum_q, sum_k = lax.psum(
        (jnp.sum(q_float * q_float, axis=1), jnp.sum(k_float * k_float, axis=1)), "head"
    )
    recip_q = lax.rsqrt(sum_q / width_q + eps)
    recip_k = lax.rsqrt(sum_k / width_k + eps)
    q_norm = (q_float * recip_q[:, None] * q_gain[None, :]).astype(jnp.bfloat16)
    k_norm = (k_float * recip_k[:, None] * k_gain[None, :]).astype(jnp.bfloat16)
    here = lax.axis_index("dp")
    lengths_row = doc_lengths[0]
    ends = jnp.cumsum(lengths_row)
    starts = ends - lengths_row
    row_index = jnp.arange(seq_len, dtype=jnp.int32)
    row_doc = jnp.sum((row_index[:, None] >= ends[None, :]).astype(jnp.int32), axis=1)
    picker = (
        row_doc[:, None] == jnp.arange(lengths_row.shape[0], dtype=jnp.int32)[None, :]
    ).astype(jnp.int32)
    row_dest = jnp.sum(picker * plan_dest[0][None, :], axis=1)
    row_start = jnp.sum(picker * starts[None, :], axis=1)
    row_shift = jnp.sum(picker * plan_offset[0][None, :], axis=1)
    leaving = row_dest != here
    target = jnp.where(leaving, row_dest * slot + row_shift + row_index - row_start, span)
    staying = jnp.logical_not(leaving)
    rank = jnp.cumsum(staying.astype(jnp.int32)) - 1
    home_index = (
        jnp.zeros((home_count,), jnp.int32)
        .at[jnp.where(staying, rank, home_count)]
        .set(row_index, mode="drop")
    )

    def to_slots(rows):
        empty = jnp.zeros((span, rows.shape[1]), rows.dtype)
        return empty.at[target].set(rows, mode="drop").reshape(devices, slot, rows.shape[1])

    present = (
        jnp.zeros((span,), jnp.bfloat16)
        .at[target]
        .set(jnp.ones((seq_len,), jnp.bfloat16), mode="drop")
        .reshape(devices, slot)
    )
    got_q, got_k, got_v, got_grad, got_present = (
        lax.all_to_all(to_slots(q_norm), "dp", split_axis=0, concat_axis=0, tiled=True),
        lax.all_to_all(to_slots(k_norm), "dp", split_axis=0, concat_axis=0, tiled=True),
        lax.all_to_all(to_slots(v_proj), "dp", split_axis=0, concat_axis=0, tiled=True),
        lax.all_to_all(to_slots(d_out), "dp", split_axis=0, concat_axis=0, tiled=True),
        lax.all_to_all(present, "dp", split_axis=0, concat_axis=0, tiled=True),
    )
    home_tags = jnp.take(row_doc, home_index)
    home_q, home_k, home_v, home_log = block_backward(
        jnp.take(q_norm, home_index, axis=0),
        jnp.take(k_norm, home_index, axis=0),
        jnp.take(v_proj, home_index, axis=0),
        jnp.take(d_out, home_index, axis=0),
        home_tags,
        home_tags,
        home_index,
        home_index,
        head_dim,
    )
    span_index = jnp.arange(span, dtype=jnp.int32)
    away_tags = jnp.where(got_present.reshape(span) > 0, span_index // slot, -1)
    per_tile = 1
    while slot * per_tile < 128 and devices % (2 * per_tile) == 0:
        per_tile = per_tile * 2
    tile_rows = slot * per_tile
    tile_count = span // tile_rows
    per_group = 1
    while tile_rows * per_group < 512 and tile_count % (2 * per_group) == 0:
        per_group = per_group * 2
    group_count = tile_count // per_group

    def grouped(values):
        return values.reshape((group_count, per_group, tile_rows) + values.shape[1:])

    def run_tile(q_rows, k_rows, v_rows, g_rows, tags, positions):
        return block_backward(
            q_rows, k_rows, v_rows, g_rows, tags, tags, positions, positions, head_dim
        )

    def tile_group(pieces):
        return jax.vmap(run_tile)(*pieces)

    results = lax.map(
        tile_group,
        (
            grouped(got_q.reshape(span, -1)),
            grouped(got_k.reshape(span, -1)),
            grouped(got_v.reshape(span, -1)),
            grouped(got_grad.reshape(span, -1)),
            grouped(away_tags),
            grouped(span_index),
        ),
    )
    away_q = results[0].reshape(span, -1).astype(jnp.bfloat16).reshape(devices, slot, -1)
    away_k = results[1].reshape(span, -1).astype(jnp.bfloat16).reshape(devices, slot, -1)
    away_v = results[2].reshape(span, -1).astype(jnp.bfloat16).reshape(devices, slot, -1)
    heads_local = results[3].shape[2]
    away_log = jnp.transpose(results[3], (2, 0, 1, 3)).reshape(heads_local, span)
    back_q_rows, back_k_rows, back_v_rows = (
        lax.all_to_all(away_q, "dp", split_axis=0, concat_axis=0, tiled=True),
        lax.all_to_all(away_k, "dp", split_axis=0, concat_axis=0, tiled=True),
        lax.all_to_all(away_v, "dp", split_axis=0, concat_axis=0, tiled=True),
    )
    picked = jnp.clip(target, 0, span - 1)
    home_spot = jnp.clip(rank, 0, home_count - 1)
    moving = leaving[:, None]
    dq_norm = jnp.where(
        moving,
        jnp.take(back_q_rows.reshape(span, -1), picked, axis=0),
        jnp.take(home_q.astype(jnp.bfloat16), home_spot, axis=0),
    )
    dk_norm = jnp.where(
        moving,
        jnp.take(back_k_rows.reshape(span, -1), picked, axis=0),
        jnp.take(home_k.astype(jnp.bfloat16), home_spot, axis=0),
    )
    grad_v = jnp.where(
        moving,
        jnp.take(back_v_rows.reshape(span, -1), picked, axis=0),
        jnp.take(home_v.astype(jnp.bfloat16), home_spot, axis=0),
    )
    balanced = jnp.concatenate([home_log, away_log], axis=1)
    scaled_q = dq_norm.astype(jnp.float32) * q_gain[None, :]
    scaled_k = dk_norm.astype(jnp.float32) * k_gain[None, :]
    back_q, back_k = lax.psum(
        (jnp.sum(scaled_q * q_float, axis=1), jnp.sum(scaled_k * k_float, axis=1)), "head"
    )
    cube_q = recip_q * recip_q * recip_q * back_q / width_q
    cube_k = recip_k * recip_k * recip_k * back_k / width_k
    grad_q = (recip_q[:, None] * scaled_q - q_float * cube_q[:, None]).astype(jnp.bfloat16)
    grad_k = (recip_k[:, None] * scaled_k - k_float * cube_k[:, None]).astype(jnp.bfloat16)
    return (grad_q, grad_k, grad_v, balanced)


def solution(mesh):
    in_specs = (
        P("dp", "head"),
        P("dp", "head"),
        P("dp", "head"),
        P("dp", "head"),
        P("head"),
        P("head"),
        P("dp", None),
        P("dp", None),
        P("dp", None),
    )
    out_specs = (P("dp", "head"), P("dp", "head"), P("dp", "head"), P("head", "dp"))
    return jax.shard_map(local, mesh=mesh, in_specs=in_specs, out_specs=out_specs, check_vma=False)
```

profile of v0, /device:TPU:2, one launch (start us, length us, event | category | flops | bytes accessed | tf_op | source)
XLA Modules:
  0.0 579.7 jit_solution(18150293846616128605)
XLA Ops:
  6.3 11.1 %scatter_custom_fusion.1 = bf16[3072]{0:T(1024)(128)(2,1)S(1)} fusion(s32[1536]{0:T(1024)S(1)} %get-tuple-element.111, bf16[1536]{0:T(1024)(128)(2,1)S(1)} %broadcast.408, bf16[]{:T(256)} %constant.142.clone.1), kind=kCustom, calls=%fused_computation.186 | custom fusion | bytes 6146 | tf_op jit(solution)/shard_map/scatter | solution.py:116
  18.1 12.0 %all-to-all-start.1 = ((bf16[64,1,48]{2,1,0:T(2,128)(2,1)}), bf16[64,1,48]{2,1,0:T(2,128)(2,1)S(1)}, u32[]{:S(2)}, u32[]{:S(2)}) async-start(bf16[64,1,48]{2,1,0:T(2,128)(2,1)} %all_to_all.36), calls=%async_computation.1 | async-start | bytes 65536 | tf_op jit(solution)/shard_map/all_to_all | solution.py:124
  30.1 5.7 scatter_custom_fusion.3
  38.6 7.7 %all-to-all-start.3 = ((bf16[64,48,128]{2,1,0:T(8,128)(2,1)}), bf16[64,48,128]{2,1,0:T(8,128)(2,1)}, u32[]{:S(2)}, u32[]{:S(2)}) async-start(bf16[64,48,128]{2,1,0:T(8,128)(2,1)} %bitcast.47), calls=%async_computation.3 | async-start | bytes 1572864 | tf_op jit(solution)/shard_map/all_to_all | solution.py:122
  47.1 17.2 %all-reduce.1 = (f32[1536]{0:T(1024)S(1)}, f32[1536]{0:T(1024)S(1)}) all-reduce(f32[1536]{0:T(1024)S(1)} %fusion.41, f32[1536]{0:T(1024)S(1)} %fusion.77), channel_id=1, replica_groups=mesh['dp'=64,'head'=4] {'head'}, use_global_device_ids=true, to_apply=%region_1.0 | all-reduce | flops 3072 | bytes 24576 | tf_op jit(solution)/shard_map/psum | solution.py:80
  64.3 6.1 %scatter_custom_fusion = bf16[3072,128]{1,0:T(8,128)(2,1)} fusion(s32[1536]{0:T(1024)S(1)} %get-tuple-element.111, bf16[]{:T(256)} %constant.142.clone.1, bf16[1536,128]{1,0:T(8,128)(2,1)S(1)} %copy-done.5, f32[128]{0:T(128)S(1)} %copy-done.28, f32[1536]{0:T(1024)S(1)} %add_rsqrt_fusion), kind=kCustom, calls=%fused_computation.124 | custom fusion | flops 786432 | bytes 1188354 | tf_op jit(solution)/shard_map/scatter | solution.py:111
  70.4 10.5 %all-to-all-start = ((bf16[64,48,128]{2,1,0:T(8,128)(2,1)}), bf16[64,48,128]{2,1,0:T(8,128)(2,1)}, u32[]{:S(2)}, u32[]{:S(2)}) async-start(bf16[64,48,128]{2,1,0:T(8,128)(2,1)} %bitcast.43), calls=%async_computation | async-start | bytes 1572864 | tf_op jit(solution)/shard_map/all_to_all | solution.py:121
  80.9 10.4 %scatter_custom_fusion.4 = bf16[3072,640]{1,0:T(8,128)(2,1)} fusion(s32[1536]{0:T(1024)S(1)} %get-tuple-element.111, bf16[1536,640]{1,0:T(8,128)(2,1)} %param.22, bf16[]{:T(256)} %constant.142.clone.1), kind=kCustom, calls=%fused_computation.86 | custom fusion | bytes 3932672 | tf_op jit(solution)/shard_map/scatter | solution.py:111
  91.3 12.7 %all-to-all-done = bf16[64,48,128]{2,1,0:T(8,128)(2,1)} async-done(((bf16[64,48,128]{2,1,0:T(8,128)(2,1)}), bf16[64,48,128]{2,1,0:T(8,128)(2,1)}, u32[]{:S(2)}, u32[]{:S(2)}) %all-to-all-start) | async-done | bytes 786464 | tf_op jit(solution)/shard_map/all_to_all | solution.py:121
  104.0 6.1 %all-to-all-start.4 = ((bf16[64,48,640]{2,1,0:T(8,128)(2,1)}), bf16[64,48,640]{2,1,0:T(8,128)(2,1)}, u32[]{:S(2)}, u32[]{:S(2)}) async-start(bf16[64,48,640]{2,1,0:T(8,128)(2,1)} %bitcast.331), calls=%async_computation.4 | async-start | bytes 7864320 | tf_op jit(solution)/shard_map/all_to_all | solution.py:123
  110.2 10.7 %scatter_custom_fusion.2 = bf16[3072,640]{1,0:T(8,128)(2,1)} fusion(s32[1536]{0:T(1024)S(1)} %get-tuple-element.111, bf16[]{:T(256)} %constant.142.clone.1, bf16[1536,640]{1,0:T(8,128)(2,1)S(1)} %copy-done, f32[640]{0:T(1024)S(1)} %copy-done.19, f32[1536]{0:T(1024)S(1)} %add_rsqrt_fusion.1), kind=kCustom, calls=%fused_computation.88 | custom fusion | flops 3932160 | bytes 5910530 | tf_op jit(solution)/shard_map/scatter | solution.py:111
  120.8 79.8 %all-to-all-done.4 = bf16[64,48,640]{2,1,0:T(8,128)(2,1)} async-done(((bf16[64,48,640]{2,1,0:T(8,128)(2,1)}), bf16[64,48,640]{2,1,0:T(8,128)(2,1)}, u32[]{:S(2)}, u32[]{:S(2)}) %all-to-all-start.4) | async-done | bytes 3932192 | tf_op jit(solution)/shard_map/all_to_all | solution.py:123
  200.6 6.2 %all-to-all-start.2 = ((bf16[64,48,640]{2,1,0:T(8,128)(2,1)}), bf16[64,48,640]{2,1,0:T(8,128)(2,1)}, u32[]{:S(2)}, u32[]{:S(2)}) async-start(bf16[64,48,640]{2,1,0:T(8,128)(2,1)} %bitcast.330), calls=%async_computation.2 | async-start | bytes 7864320 | tf_op jit(solution)/shard_map/all_to_all | solution.py:120
  207.2 90.1 %all-to-all-done.2 = bf16[64,48,640]{2,1,0:T(8,128)(2,1)} async-done(((bf16[64,48,640]{2,1,0:T(8,128)(2,1)}), bf16[64,48,640]{2,1,0:T(8,128)(2,1)}, u32[]{:S(2)}, u32[]{:S(2)}) %all-to-all-start.2) | async-done | bytes 3932192 | tf_op jit(solution)/shard_map/all_to_all | solution.py:120
  297.3 94.9 %while.16 = (s32[]{:T(128)}, bf16[4,4,192,640]{3,2,1,0:T(8,128)(2,1)}, bf16[4,4,192,128]{3,2,1,0:T(8,128)(2,1)}, bf16[4,4,192,128]{3,2,1,0:T(8,128)(2,1)}, f32[4...) while((s32[]{:T(128)}, ...), condition=%wide.region_18.19_spmd, body=%wide.region_14.18_spmd.sunk | while | flops 1153220352 | bytes 68116280 | solution.py:161
  392.2 28.6 %all_to_all.45 = bf16[64,48,128]{2,1,0:T(8,128)(2,1)S(1)} all-to-all(bf16[64,48,128]{2,1,0:T(8,128)(2,1)} %bitcast.338), channel_id=1, replica_groups=mesh['dp'=64,'head'=4] {'dp'}, dimensions={0} | all-to-all | bytes 1572864 | tf_op jit(solution)/shard_map/all_to_all | solution.py:179
  420.8 29.1 %all_to_all.46 = bf16[64,48,128]{2,1,0:T(8,128)(2,1)} all-to-all(bf16[64,48,128]{2,1,0:T(8,128)(2,1)} %bitcast.337), channel_id=1, replica_groups=mesh['dp'=64,'head'=4] {'dp'}, dimensions={0} | all-to-all | bytes 1572864 | tf_op jit(solution)/shard_map/all_to_all | solution.py:180
  449.9 6.2 %all-to-all-start.5 = ((bf16[64,48,640]{2,1,0:T(8,128)(2,1)}), bf16[64,48,640]{2,1,0:T(8,128)(2,1)}, u32[]{:S(2)}, u32[]{:S(2)}) async-start(bf16[64,48,640]{2,1,0:T(8,128)(2,1)} %bitcast.334), calls=%async_computation.5 | async-start | bytes 7864320 | tf_op jit(solution)/shard_map/all_to_all | solution.py:178
  456.1 6.2 %scatter_custom_fusion.5 = s32[384]{0:T(512)S(1)} fusion(s32[1536]{0:T(1024)S(1)} %get-tuple-element.109, s32[1536]{0:T(1024)S(1)} %iota.75, s32[]{:T(128)} %constant.130.clone.1), kind=kCustom, calls=%fused_computation.191 | custom fusion | bytes 1540 | tf_op jit(solution)/shard_map/scatter | solution.py:106
  467.7 4.5 gather_fusion.6
  514.2 5.8 gather_fusion.2
  546.6 8.7 %gather_fusion = bf16[1536,640]{1,0:T(8,128)(2,1)} fusion(bf16[3072,640]{1,0:T(8,128)(2,1)} %bitcast.52, s32[2048]{0:T(1024)} %pad_clamp_fusion.3), kind=kCustom, calls=%fused_computation.8 | custom fusion | bytes 3938304 | tf_op jit(solution)/shard_map/jit(_take)/gather | solution.py:187
  555.3 5.3 fusion.44
  560.7 14.3 %all-reduce = (f32[1536]{0:T(1024)S(1)}, f32[1536]{0:T(1024)S(1)}) all-reduce(f32[1536]{0:T(1024)S(1)} %get-tuple-element.142, f32[1536]{0:T(1024)S(1)} %get-tuple-element.140), channel_id=1, replica_groups=mesh['dp'=64,'head'=4] {'head'}, use_global_device_ids=true, to_apply=%region_26.29 | all-reduce | flops 3072 | bytes 24576 | tf_op jit(solution)/shard_map/psum | solution.py:203
  (245 shorter events, 182.8 us)
Async XLA Ops:
  0.6 45.7 %copy-start.5 = (bf16[1536,128]{1,0:T(8,128)(2,1)S(1)}, bf16[1536,128]{1,0:T(8,128)(2,1)}, u32[]{:S(2)}) copy-start(bf16[1536,128]{1,0:T(8,128)(2,1)} %param.20) | copy-start | bytes 1179652
  0.6 46.0 %copy-start = (bf16[1536,640]{1,0:T(8,128)(2,1)S(1)}, bf16[1536,640]{1,0:T(8,128)(2,1)}, u32[]{:S(2)}) copy-start(bf16[1536,640]{1,0:T(8,128)(2,1)} %param.19) | copy-start | bytes 5898244
  0.7 63.6 %copy-start.28 = (f32[128]{0:T(128)S(1)}, f32[128]{0:T(128)}, u32[]{:S(2)}) copy-start(f32[128]{0:T(128)} %param.24) | copy-start | bytes 1540
  4.0 14.1 %copy-start.17 = (pred[1536]{0:T(1024)(128)(4,1)}, pred[1536]{0:T(1024)(128)(4,1)S(1)}, u32[]{:S(2)}) copy-start(pred[1536]{0:T(1024)(128)(4,1)S(1)} %get-tuple-element.147) | copy-start | bytes 4612
  18.1 20.5 %all-to-all-start.1 = ((bf16[64,1,48]{2,1,0:T(2,128)(2,1)}), bf16[64,1,48]{2,1,0:T(2,128)(2,1)S(1)}, u32[]{:S(2)}, u32[]{:S(2)}) async-start(bf16[64,1,48]{2,1,0:T(2,128)(2,1)} %all_to_all.36), calls=%async_computation.1 | async-start | bytes 65536 | tf_op jit(solution)/shard_map/all_to_all | solution.py:124
  38.6 31.8 %all-to-all-start.3 = ((bf16[64,48,128]{2,1,0:T(8,128)(2,1)}), bf16[64,48,128]{2,1,0:T(8,128)(2,1)}, u32[]{:S(2)}, u32[]{:S(2)}) async-start(bf16[64,48,128]{2,1,0:T(8,128)(2,1)} %bitcast.47), calls=%async_computation.3 | async-start | bytes 1572864 | tf_op jit(solution)/shard_map/all_to_all | solution.py:122
  64.2 27.1 %copy-start.25 = (f32[1536]{0:T(1024)}, f32[1536]{0:T(1024)S(1)}, u32[]{:S(2)}) copy-start(f32[1536]{0:T(1024)S(1)} %get-tuple-element.137) | copy-start | bytes 18436
  64.2 45.9 %copy-start.23 = (f32[1536]{0:T(1024)}, f32[1536]{0:T(1024)S(1)}, u32[]{:S(2)}) copy-start(f32[1536]{0:T(1024)S(1)} %get-tuple-element.136) | copy-start | bytes 18436
  70.4 33.6 %all-to-all-start = ((bf16[64,48,128]{2,1,0:T(8,128)(2,1)}), bf16[64,48,128]{2,1,0:T(8,128)(2,1)}, u32[]{:S(2)}, u32[]{:S(2)}) async-start(bf16[64,48,128]{2,1,0:T(8,128)(2,1)} %bitcast.43), calls=%async_computation | async-start | bytes 1572864 | tf_op jit(solution)/shard_map/all_to_all | solution.py:121
  104.0 6.1 %copy-start.19 = (f32[640]{0:T(1024)S(1)}, f32[640]{0:T(1024)}, u32[]{:S(2)}) copy-start(f32[640]{0:T(1024)} %param.23) | copy-start | bytes 7684
  104.0 96.6 %all-to-all-start.4 = ((bf16[64,48,640]{2,1,0:T(8,128)(2,1)}), bf16[64,48,640]{2,1,0:T(8,128)(2,1)}, u32[]{:S(2)}, u32[]{:S(2)}) async-start(bf16[64,48,640]{2,1,0:T(8,128)(2,1)} %bitcast.331), calls=%async_computation.4 | async-start | bytes 7864320 | tf_op jit(solution)/shard_map/all_to_all | solution.py:123
  200.6 96.7 %all-to-all-start.2 = ((bf16[64,48,640]{2,1,0:T(8,128)(2,1)}), bf16[64,48,640]{2,1,0:T(8,128)(2,1)}, u32[]{:S(2)}, u32[]{:S(2)}) async-start(bf16[64,48,640]{2,1,0:T(8,128)(2,1)} %bitcast.330), calls=%async_computation.2 | async-start | bytes 7864320 | tf_op jit(solution)/shard_map/all_to_all | solution.py:120
  449.9 96.7 %all-to-all-start.5 = ((bf16[64,48,640]{2,1,0:T(8,128)(2,1)}), bf16[64,48,640]{2,1,0:T(8,128)(2,1)}, u32[]{:S(2)}, u32[]{:S(2)}) async-start(bf16[64,48,640]{2,1,0:T(8,128)(2,1)} %bitcast.334), calls=%async_computation.5 | async-start | bytes 7864320 | tf_op jit(solution)/shard_map/all_to_all | solution.py:178
  464.8 7.4 %copy-start.1 = (bf16[1536,640]{1,0:T(8,128)(2,1)S(1)}, bf16[1536,640]{1,0:T(8,128)(2,1)}, u32[]{:S(2)}) copy-start(bf16[1536,640]{1,0:T(8,128)(2,1)} %param.19) | copy-start | bytes 5898244
  506.1 8.1 %copy-start.27 = (s32[1536]{0:T(1024)S(1)}, s32[1536]{0:T(1024)}, u32[]{:S(2)}) copy-start(s32[1536]{0:T(1024)} %get-tuple-element.108) | copy-start | bytes 18436
  519.9 11.8 %copy-start.3 = (bf16[64,48,128]{2,1,0:T(8,128)(2,1)S(1)}, bf16[64,48,128]{2,1,0:T(8,128)(2,1)}, u32[]{:S(2)}) copy-start(bf16[64,48,128]{2,1,0:T(8,128)(2,1)} %all_to_all.46) | copy-start | bytes 2359300
  531.8 7.4 %copy-start.9 = (bf16[1536,128]{1,0:T(8,128)(2,1)S(1)}, bf16[1536,128]{1,0:T(8,128)(2,1)}, u32[]{:S(2)}) copy-start(bf16[1536,128]{1,0:T(8,128)(2,1)} %gather_fusion.10) | copy-start | bytes 1179652
  546.6 8.7 %copy-start.18 = (pred[1536]{0:T(1024)(128)(4,1)S(1)}, pred[1536]{0:T(1024)(128)(4,1)}, u32[]{:S(2)}) copy-start(pred[1536]{0:T(1024)(128)(4,1)} %copy-done.17) | copy-start | bytes 4612
  546.6 8.7 %copy-start.20 = (f32[640]{0:T(1024)S(1)}, f32[640]{0:T(1024)}, u32[]{:S(2)}) copy-start(f32[640]{0:T(1024)} %param.23) | copy-start | bytes 7684
  546.6 8.7 %copy-start.21 = (pred[1536]{0:T(1024)(128)(4,1)S(1)}, pred[1536]{0:T(1024)(128)(4,1)}, u32[]{:S(2)}) copy-start(pred[1536]{0:T(1024)(128)(4,1)} %get-tuple-element.144) | copy-start | bytes 4612
  546.6 8.7 %copy-start.22 = (pred[1536]{0:T(1024)(128)(4,1)S(1)}, pred[1536]{0:T(1024)(128)(4,1)}, u32[]{:S(2)}) copy-start(pred[1536]{0:T(1024)(128)(4,1)} %get-tuple-element.148) | copy-start | bytes 4612
  555.3 19.6 %copy-start.24 = (f32[1536]{0:T(1024)S(1)}, f32[1536]{0:T(1024)}, u32[]{:S(2)}) copy-start(f32[1536]{0:T(1024)} %copy-done.23) | copy-start | bytes 18436
  555.3 19.6 %copy-start.26 = (f32[1536]{0:T(1024)S(1)}, f32[1536]{0:T(1024)}, u32[]{:S(2)}) copy-start(f32[1536]{0:T(1024)} %copy-done.25) | copy-start | bytes 18436
  555.3 19.7 %copy-start.29 = (f32[128]{0:T(128)S(1)}, f32[128]{0:T(128)}, u32[]{:S(2)}) copy-start(f32[128]{0:T(128)} %param.24) | copy-start | bytes 1540
  (29 other events, 68.2 us)
where the time goes:
time: 590 us; the launch traced here: 580 us
  waiting for transfers between devices  190 us (32%)
  local copies, waits for them, and re-layouts  136 us (23%)
  blocking collectives  89.2 us (15%)
  other arithmetic  57.3 us (10%)
  matrix products  56.7 us (10%)
  starting transfers between devices  48.6 us (8%)
    all_to_all x1, waiting for transfers between devices, local(): lax.all_to_all(to_slots(q_norm), 'dp', split_axis=0, concat_axis=0, tiled...  90.1 us
    all_to_all x1, waiting for transfers between devices, local(): lax.all_to_all(to_slots(d_out), 'dp', split_axis=0, concat_axis=0, tiled=...  79.8 us
    all_to_all x1, blocking collectives, local(): lax.all_to_all(away_v, 'dp', split_axis=0, concat_axis=0, tiled=True)  29.1 us
    all_to_all x1, blocking collectives, local(): lax.all_to_all(away_k, 'dp', split_axis=0, concat_axis=0, tiled=True)  28.6 us
    dynamic_slice x12, local copies, waits for them, and re-layouts, local(): lax.map(tile_group, (grouped(got_q.reshape(span, -1)), grouped(got_k.resh...  19 us
    psum x1, blocking collectives, local(): lax.psum((jnp.sum(q_float * q_float, axis=1), jnp.sum(k_float * k_float,...  17.2 us
    scatter x2, other arithmetic, to_slots(): empty.at[target].set(rows, mode='drop')  16.8 us
    scatter x2, local copies, waits for them, and re-layouts, to_slots(): empty.at[target].set(rows, mode='drop')  16.2 us
  transfers between devices with their start and end apart: 6, of which 5 were waited for; matrix products, arithmetic and copies ran while one was open for 21% of the time, Pallas kernels for 0%

commit v1 on v0

v1 whole, which is shorter than its diff:
```python
import functools
import math

import jax
import jax.numpy as jnp
from jax import lax
from jax.experimental import pallas as pl
from jax.experimental.pallas import tpu as pltpu
from jax.sharding import PartitionSpec as P

HDIM = 128
TILE = 128
SEQ = 1536
TILES = SEQ // TILE
GROUP = 5
DOCS = 36
DEVICES = 64
SLOT = 48
HOME = 384
REACH = 4
WIDTH_Q = 2560
WIDTH_K = 512

eps = 1e-06
big_negative = -1e30
scaling = 1.0 / math.sqrt(HDIM)
log2e = math.log2(math.e)
to_exp2 = scaling * log2e

f32 = jnp.float32
bf16 = jnp.bfloat16

VMEM = pl.BlockSpec(memory_space=pltpu.VMEM)
SMEM = pl.BlockSpec(memory_space=pltpu.SMEM)

mxu_nt = functools.partial(
    lax.dot_general, dimension_numbers=(((1,), (1,)), ((), ())), preferred_element_type=f32
)
mxu_nn = functools.partial(
    lax.dot_general, dimension_numbers=(((1,), (0,)), ((), ())), preferred_element_type=f32
)
mxu_tn = functools.partial(
    lax.dot_general, dimension_numbers=(((0,), (0,)), ((), ())), preferred_element_type=f32
)


def call(kernel, outs, ins, out_specs=None, scratch=(), flops=10**7, name=None):
    shapes = [jax.ShapeDtypeStruct(s, d) for s, d in outs]
    return pl.pallas_call(
        kernel,
        out_shape=shapes,
        in_specs=ins,
        out_specs=out_specs or [VMEM] * len(outs),
        scratch_shapes=list(scratch),
        compiler_params=pltpu.CompilerParams(vmem_limit_bytes=40 * 2**20),
        cost_estimate=pl.CostEstimate(flops=flops, bytes_accessed=10**6, transcendentals=0),
        name=name,
    )


def row_sums(values):
    return jnp.sum(jnp.transpose(values), axis=0, keepdims=True)


def fold(values):
    total = values[:, :HDIM]
    for h in range(1, values.shape[1] // HDIM):
        total = total + values[:, h * HDIM : (h + 1) * HDIM]
    return total


def square_kernel(q_ref, k_ref, out_ref):
    for i in range(TILES):
        rows = pl.ds(i * TILE, TILE)
        q = q_ref[rows, :].astype(f32)
        k = k_ref[rows, :].astype(f32)
        out_ref[i : i + 1, :] = row_sums(fold(q * q))
        out_ref[TILES + i : TILES + i + 1, :] = row_sums(k * k)


def layout_kernel(len_ref, start_ref, low_ref):
    rows = start_ref.shape[0]
    position = lax.broadcasted_iota(jnp.int32, (rows, TILE), 0) * TILE + lax.broadcasted_iota(
        jnp.int32, (rows, TILE), 1
    )
    zero = jnp.int32(0)

    def step(j, carry):
        end, start, lows = carry
        end = end + len_ref[0, j]
        start = jnp.where(position >= end, end, start)
        lows = tuple(jnp.where(end <= i * TILE, end, low) for i, low in enumerate(lows))
        return end, start, lows

    _, start, lows = lax.fori_loop(
        0, DOCS, step, (zero, jnp.zeros((rows, TILE), jnp.int32), (zero,) * TILES)
    )
    start_ref[...] = start
    for i in range(TILES):
        low_ref[i] = lows[i] // TILE


def columns_of(rows):
    stack = jnp.concatenate(rows + [jnp.zeros((8 - len(rows), TILE), f32)], axis=0)
    turned = jnp.transpose(stack)
    return [turned[:, j : j + 1] for j in range(len(rows))]


def allowed_of(start_row, low, tile, count):
    key = low * TILE + lax.broadcasted_iota(jnp.int32, (count * TILE, TILE), 0)
    query = tile * TILE + lax.broadcasted_iota(jnp.int32, (count * TILE, TILE), 1)
    return (key >= start_row) & (key <= query)


def forward_kernel(
    me_ref, low_ref, len_ref, dest_ref, shift_ref, start_ref,
    q_ref, k_ref, qg_ref, kg_ref, s0_ref, s1_ref, s2_ref, s3_ref,
    qn_ref, kn_ref, recip_ref, lse_ref, slot_ref, home_ref,
):
    total = s0_ref[...] + s1_ref[...] + s2_ref[...] + s3_ref[...]
    recip_ref[:TILES, :] = lax.rsqrt(total[:TILES] * (1.0 / WIDTH_Q) + eps)
    recip_ref[TILES:, :] = lax.rsqrt(total[TILES:] * (1.0 / WIDTH_K) + eps)
    slot_ref[...] = jnp.zeros(slot_ref.shape, f32)
    home_ref[...] = jnp.zeros(home_ref.shape, f32)
    lse_ref[TILES:] = jnp.zeros((lse_ref.shape[0] - TILES, 8, TILE), f32)

    def tile_step(i, carry):
        rows = pl.ds(pl.multiple_of(i * TILE, TILE), TILE)
        col_q, col_k = columns_of([recip_ref[pl.ds(i, 1), :], recip_ref[pl.ds(TILES + i, 1), :]])
        kn_ref[rows, :] = (k_ref[rows, :].astype(f32) * col_k * kg_ref[...]).astype(bf16)
        qn_ref[rows, :] = (q_ref[rows, :].astype(f32) * col_q * qg_ref[...]).astype(bf16)
        low = low_ref[i]
        count_here = i - low + 1
        start_row = start_ref[pl.ds(i, 1), :]

        for count in range(1, REACH + 1):

            @pl.when(count_here == count)
            def _(count=count):
                keys = kn_ref[pl.ds(pl.multiple_of(low * TILE, TILE), count * TILE), :]
                allowed = allowed_of(start_row, low, i, count)
                logs = []
                for h in range(GROUP):
                    raw = mxu_nt(keys, qn_ref[rows, h * HDIM : (h + 1) * HDIM])
                    masked = jnp.where(allowed, raw, big_negative)
                    peak = jnp.max(masked, axis=0, keepdims=True)
                    grown = jnp.exp2((masked - peak) * to_exp2)
                    logs.append(
                        peak * scaling + jnp.log(jnp.sum(grown, axis=0, keepdims=True))
                    )
                logs.append(jnp.zeros((8 - GROUP, TILE), f32))
                lse_ref[pl.ds(i, 1)] = jnp.concatenate(logs, axis=0)[None]

        return carry

    lax.fori_loop(0, TILES, tile_step, 0)

    me = me_ref[0]
    lane = lax.broadcasted_iota(jnp.int32, (8, TILE), 1)

    def doc_step(j, carry):
        start, kept = carry
        length = len_ref[0, j]
        dest = dest_ref[0, j]
        stays = dest == me

        @pl.when(jnp.logical_not(stays))
        def _():
            block = start // TILE
            inner = start % TILE
            place = (me * SLOT + shift_ref[0, j]) % TILE
            turn = (place - inner + TILE) % TILE
            here = pltpu.roll(lse_ref[block], turn, 1)
            after = pltpu.roll(lse_ref[block + 1], turn, 1)
            index = (lane - place) & (TILE - 1)
            value = jnp.where(index < TILE - inner, here, after)
            slot_ref[dest] = jnp.where(index < length, value, 0.0)

        @pl.when(stays)
        def _():
            gap = start - kept
            block = gap // TILE
            inner = gap % TILE
            turn = (TILE - inner) % TILE
            for b in range(HOME // TILE):
                here = pltpu.roll(lse_ref[block + b], turn, 1)
                after = pltpu.roll(lse_ref[block + b + 1], turn, 1)
                value = jnp.where(lane < TILE - inner, here, after)
                column = lane + b * TILE
                inside = (column >= kept) & (column < kept + length)
                part = slice(b * TILE, (b + 1) * TILE)
                home_ref[:, part] = jnp.where(inside, value, home_ref[:, part])

        return start + length, jnp.where(stays, kept + length, kept)

    lax.fori_loop(0, DOCS, doc_step, (jnp.int32(0), jnp.int32(0)))


def backward_kernel(
    low_ref, start_ref, qn_ref, kn_ref, v_ref, g_ref, lse_ref, q_ref, k_ref, qg_ref, kg_ref,
    dq_ref, dk_ref, dv_ref, sums_ref, dk_acc, dv_acc,
):
    dk_acc[...] = jnp.zeros(dk_acc.shape, f32)
    dv_acc[...] = jnp.zeros(dv_acc.shape, f32)

    def tile_step(i, carry):
        rows = pl.ds(pl.multiple_of(i * TILE, TILE), TILE)
        low = low_ref[i]
        count_here = i - low + 1
        start_row = start_ref[pl.ds(i, 1), :]

        for count in range(1, REACH + 1):

            @pl.when(count_here == count)
            def _(count=count):
                window = pl.ds(pl.multiple_of(low * TILE, TILE), count * TILE)
                keys = kn_ref[window, :]
                values = v_ref[window, :]
                allowed = allowed_of(start_row, low, i, count)
                logs = lse_ref[i] * log2e
                lows, grads, qs, gs = [], [], [], []
                for h in range(GROUP):
                    head = slice(h * HDIM, (h + 1) * HDIM)
                    q = qn_ref[rows, head]
                    g = g_ref[rows, head]
                    raw = mxu_nt(keys, q)
                    weights = jnp.where(
                        allowed, jnp.exp2(raw * to_exp2 - logs[h : h + 1, :]), 0.0
                    )
                    low_weights = weights.astype(bf16)
                    grad_weights = mxu_nt(values, g)
                    delta = jnp.sum(
                        low_weights.astype(f32) * grad_weights, axis=0, keepdims=True
                    )
                    grad = (weights * (grad_weights - delta) * scaling).astype(bf16)
                    lows.append(low_weights)
                    grads.append(grad)
                    qs.append(q)
                    gs.append(g)
                low_all = jnp.concatenate(lows, axis=1)
                grad_all = jnp.concatenate(grads, axis=1)
                dv_acc[window, :] += mxu_nn(low_all, jnp.concatenate(gs, axis=0))
                dk_acc[window, :] += mxu_nn(grad_all, jnp.concatenate(qs, axis=0))
                dq = mxu_tn(grad_all, keys).astype(bf16)
                for h in range(GROUP):
                    dq_ref[rows, h * HDIM : (h + 1) * HDIM] = dq[h * TILE : (h + 1) * TILE]

        scaled = dq_ref[rows, :].astype(f32) * qg_ref[...]
        sums_ref[pl.ds(i, 1), :] = row_sums(fold(scaled * q_ref[rows, :].astype(f32)))
        return carry

    lax.fori_loop(0, TILES, tile_step, 0)
    dk = dk_acc[...].astype(bf16)
    dk_ref[...] = dk
    dv_ref[...] = dv_acc[...].astype(bf16)
    scaled = dk.astype(f32) * kg_ref[...] * k_ref[...].astype(f32)
    for i in range(TILES):
        sums_ref[TILES + i : TILES + i + 1, :] = row_sums(scaled[i * TILE : (i + 1) * TILE])


def norm_kernel(
    q_ref, k_ref, dq_ref, dk_ref, qg_ref, kg_ref, recip_ref, s0_ref, s1_ref, s2_ref, s3_ref,
    gq_ref, gk_ref,
):
    recip = recip_ref[...]
    cube = recip * recip * recip * (s0_ref[...] + s1_ref[...] + s2_ref[...] + s3_ref[...])
    for i in range(TILES):
        rows = pl.ds(i * TILE, TILE)
        at_q, at_k = slice(i, i + 1), slice(TILES + i, TILES + i + 1)
        r_q, c_q, r_k, c_k = columns_of(
            [
                recip[at_q],
                cube[at_q] * (1.0 / WIDTH_Q),
                recip[at_k],
                cube[at_k] * (1.0 / WIDTH_K),
            ]
        )
        scaled = dq_ref[rows, :].astype(f32) * qg_ref[...]
        gq_ref[rows, :] = (r_q * scaled - q_ref[rows, :].astype(f32) * c_q).astype(bf16)
        scaled = dk_ref[rows, :].astype(f32) * kg_ref[...]
        gk_ref[rows, :] = (r_k * scaled - k_ref[rows, :].astype(f32) * c_k).astype(bf16)


def assemble_kernel(got_ref, home_ref, out_ref):
    out_ref[:, :HOME] = home_ref[:GROUP, :]
    lane = lax.broadcasted_iota(jnp.int32, (8, TILE), 1)
    for b in range(DEVICES * SLOT // TILE):
        total = None
        for s in range(b * TILE // SLOT, (b * TILE + TILE - 1) // SLOT + 1):
            left = s * SLOT - b * TILE
            value = got_ref[s]
            if left < 0:
                value = jnp.where(lane < left + SLOT, value, 0.0)
            if left + SLOT > TILE:
                value = jnp.where(lane >= left, value, 0.0)
            total = value if total is None else total + value
        out_ref[:, HOME + b * TILE : HOME + (b + 1) * TILE] = total[:GROUP]


def from_others(values):
    size = lax.axis_size("head")
    return [values] + [
        lax.ppermute(values, "head", [(i, (i + s) % size) for i in range(size)])
        for s in range(1, size)
    ]


def local(q_raw, k_raw, v_proj, d_out, q_gain, k_gain, doc_lengths, plan_dest, plan_offset):
    me = lax.axis_index("dp").astype(jnp.int32).reshape(1)
    qg = q_gain.reshape(1, -1)
    kg = k_gain.reshape(1, -1)
    stat = ((2 * TILES, TILE), f32)
    wide = ((SEQ, GROUP * HDIM), bf16)
    thin = ((SEQ, HDIM), bf16)

    (squares,) = call(square_kernel, [stat], [VMEM] * 2, name="squares")(q_raw, k_raw)
    start, low = call(
        layout_kernel,
        [((16, TILE), jnp.int32), ((TILES,), jnp.int32)],
        [SMEM],
        [VMEM, SMEM],
        name="layout",
    )(doc_lengths)
    qn, kn, recip, lse, slots, home = call(
        forward_kernel,
        [
            wide,
            thin,
            stat,
            ((16, 8, TILE), f32),
            ((DEVICES, 8, TILE), f32),
            ((8, HOME), f32),
        ],
        [SMEM] * 5 + [VMEM] * 9,
        name="forward",
    )(
        me, low, doc_lengths, plan_dest, plan_offset, start,
        q_raw, k_raw, qg, kg, *from_others(squares),
    )
    got = lax.all_to_all(slots, "dp", split_axis=0, concat_axis=0, tiled=True)
    dq, dk, grad_v, sums = call(
        backward_kernel,
        [wide, thin, thin, stat],
        [SMEM] + [VMEM] * 10,
        scratch=[pltpu.VMEM((SEQ, HDIM), f32)] * 2,
        flops=10**10,
        name="backward",
    )(low, start, qn, kn, v_proj, d_out, lse, q_raw, k_raw, qg, kg)
    grad_q, grad_k = call(norm_kernel, [wide, thin], [VMEM] * 11, name="normback")(
        q_raw, k_raw, dq, dk, qg, kg, recip, *from_others(sums)
    )
    (balanced,) = call(
        assemble_kernel, [((GROUP, HOME + DEVICES * SLOT), f32)], [VMEM] * 2, name="assemble"
    )(got, home)
    return grad_q, grad_k, grad_v, balanced


def solution(mesh):
    in_specs = (
        P("dp", "head"),
        P("dp", "head"),
        P("dp", "head"),
        P("dp", "head"),
        P("head"),
        P("head"),
        P("dp", None),
        P("dp", None),
        P("dp", None),
    )
    out_specs = (P("dp", "head"), P("dp", "head"), P("dp", "head"), P("head", "dp"))
    return jax.shard_map(local, mesh=mesh, in_specs=in_specs, out_specs=out_specs, check_vma=False)
```

time: 590 us -> 63.3 us (0.11)
  the two profiles are of different devices: /device:TPU:2 before, /device:TPU:1 now
where the time goes in v1:
time: 63.3 us; the launch traced here: 62.3 us
  Pallas kernels  29.5 us (47%)
  starting transfers between devices  20.8 us (33%)
  local copies, waits for them, and re-layouts  6.92 us (11%)
  waiting for transfers between devices  4.42 us (7%)
  between operations  0.75 us (1%)
    all_to_all x1, starting transfers between devices, local(): got = lax.all_to_all(slots, 'dp', split_axis=0, concat_axis=0, tiled=True)  13.8 us
    pallas_call x1, Pallas kernels, local(): call(backward_kernel, [wide, thin, thin, stat], [SMEM] + [VMEM] * 10, scr...  12.3 us
    pallas_call x1, Pallas kernels, local(): call(forward_kernel, [wide, thin, stat, ((16, 8, TILE), f32), ((DEVICES,...  11.2 us
    ppermute x6, starting transfers between devices, from_others(): lax.ppermute(values, 'head', [(i, (i + s) % size) for i in range(size)])  6.95 us
    unnamed x26, local copies, waits for them, and re-layouts  6.92 us
    ppermute x6, waiting for transfers between devices, from_others(): lax.ppermute(values, 'head', [(i, (i + s) % size) for i in range(size)])  4.42 us
    pallas_call x1, Pallas kernels, local(): call(norm_kernel, [wide, thin], [VMEM] * 11, name='normback')  2.92 us
    pallas_call x1, Pallas kernels, local(): call(layout_kernel, [((16, TILE), jnp.int32), ((TILES,), jnp.int32)], [SM...  1.91 us
  transfers between devices with their start and end apart: 7, of which 5 were waited for; matrix products, arithmetic and copies ran while one was open for 0% of the time, Pallas kernels for 27%

profile of v1, /device:TPU:1, one launch (start us, length us, event | category | flops | bytes accessed | tf_op | source)
XLA Modules:
  0.0 62.3 jit_solution(1165574816265822534)
XLA Ops:
  0.6 1.5 %copy-done = bf16[1536,640]{1,0:T(8,128)(2,1)S(1)} copy-done((bf16[1536,640]{1,0:T(8,128)(2,1)S(1)}, bf16[1536,640]{1,0:T(8,128)(2,1)}, u32[]{:S(2)}) %copy-start) | copy-done | bytes 1966104
  2.2 1.0 %copy-done.2 = bf16[1536,128]{1,0:T(8,128)(2,1)S(1)} copy-done((bf16[1536,128]{1,0:T(8,128)(2,1)S(1)}, bf16[1536,128]{1,0:T(8,128)(2,1)}, u32[]{:S(2)}) %copy-start.2) | copy-done | bytes 393240
  3.2 0.5 squares.1.s0_ref
  3.8 3.6 %collective-permute-start.2 = (f32[24,128]{1,0:T(8,128)S(1)}, f32[24,128]{1,0:T(8,128)S(1)}, u32[]{:S(2)}, u32[]{:S(2)}) collective-permute-start(f32[24,128]{1,0:T(8,128)S(1)} %squares.1.s0_ref), channel_id=1, source_target_pairs={{0,3},{1,0},{2,1},{3,2},{4,7},{5,4},{6,5},{7,6},{8,11},{9,8},{10,9... | collective-permute-start | bytes 36872 | tf_op jit(solution)/shard_map/ppermute | solution.py:303
  7.4 0.3 collective-permute-start.1
  7.8 0.7 %collective-permute-start = (f32[24,128]{1,0:T(8,128)S(1)}, f32[24,128]{1,0:T(8,128)S(1)}, u32[]{:S(2)}, u32[]{:S(2)}) collective-permute-start(f32[24,128]{1,0:T(8,128)S(1)} %squares.1.s0_ref), channel_id=1, source_target_pairs={{0,1},{1,2},{2,3},{3,0},{4,5},{5,6},{6,7},{7,4},{8,9},{9,10},{10,1... | collective-permute-start | bytes 36872 | tf_op jit(solution)/shard_map/ppermute | solution.py:303
  8.5 1.9 %layout.1 = (s32[16,128]{1,0:T(8,128)S(1)}, s32[12]{0:T(128)S(1)}) custom-call(s32[1,36]{1,0:T(1,128)S(1)} %copy-done.5), custom_call_target="tpu_custom_call" | custom-call | flops 10000000 | bytes 1000000 | tf_op jit(solution)/shard_map/layout/pallas_call | solution.py:317
  10.4 1.1 %collective-permute-done.1.s2_ref = f32[24,128]{1,0:T(8,128)S(1)} collective-permute-done((f32[24,128]{1,0:T(8,128)S(1)}, f32[24,128]{1,0:T(8,128)S(1)}, u32[]{:S(2)}, u32[]{:S(2)}) %collective-permute-start.1) | collective-permute-done | bytes 12320 | tf_op jit(solution)/shard_map/ppermute | solution.py:303
  11.5 0.1 collective-permute-done.s1_ref
  11.6 11.2 %forward.1 = (bf16[1536,640]{1,0:T(8,128)(2,1)S(1)}, bf16[1536,128]{1,0:T(8,128)(2,1)S(1)}, f32[24,128]{1,0:T(8,128)S(1)}, f32[16,8,128]{2,1,0:T(8,128)S(1)}, f3...) custom-call(s32[1]{0:T(128)} %bitcast.me_ref, s32[12]{0:T(128)S(1)} %get-tuple-element.18.low_ref, s32[1,36]{1,0:T(1,128)S(1)} %copy-done.5, ...), custom_call_target="tpu_custom_call" | custom-call | flops 10000000 | bytes 1000000 | tf_op jit(solution)/shard_map/forward/pallas_call | solution.py:324
  22.8 1.3 %copy-done.9 = bf16[1536,640]{1,0:T(8,128)(2,1)} copy-done((bf16[1536,640]{1,0:T(8,128)(2,1)}, bf16[1536,640]{1,0:T(8,128)(2,1)S(1)}, u32[]{:S(2)}) %copy-start.9) | copy-done | bytes 1966104
  24.1 13.8 %all-to-all-start = ((f32[64,8,128]{2,1,0:T(8,128)}), f32[64,8,128]{2,1,0:T(8,128)S(1)}, u32[]{:S(2)}, u32[]{:S(2)}) async-start(f32[64,8,128]{2,1,0:T(8,128)} %get-tuple-element.30), calls=%async_computation | async-start | bytes 524288 | tf_op jit(solution)/shard_map/all_to_all | solution.py:340
  37.9 0.0 copy-start.8
  37.9 1.5 %copy-done.8 = bf16[1536,640]{1,0:T(8,128)(2,1)S(1)} copy-done((bf16[1536,640]{1,0:T(8,128)(2,1)S(1)}, bf16[1536,640]{1,0:T(8,128)(2,1)}, u32[]{:S(2)}) %copy-start.8) | copy-done | bytes 1966104
  39.4 1.5 %copy-done.10 = bf16[1536,640]{1,0:T(8,128)(2,1)S(1)} copy-done((bf16[1536,640]{1,0:T(8,128)(2,1)S(1)}, bf16[1536,640]{1,0:T(8,128)(2,1)}, u32[]{:S(2)}) %copy-start.10) | copy-done | bytes 1966104
  41.0 12.3 %backward.1 = (bf16[1536,640]{1,0:T(8,128)(2,1)S(1)}, bf16[1536,128]{1,0:T(8,128)(2,1)S(1)}, bf16[1536,128]{1,0:T(8,128)(2,1)}, f32[24,128]{1,0:T(8,128)S(1)}) custom-call(s32[12]{0:T(128)S(1)} %get-tuple-element.18.low_ref, s32[16,128]{1,0:T(8,128)S(1)} %get-tuple-element.19.start_ref, bf16[1536,640]{1,0:T(8,128)(2,1)S(1)} %copy-done.10, ...), custom_call_target="tpu_custom_call" | custom-call | flops 10000000000 | bytes 1000000 | tf_op jit(solution)/shard_map/backward/pallas_call | solution.py:341
  53.2 0.1 collective-permute-start.5
  53.4 1.3 %collective-permute-start.4 = (f32[24,128]{1,0:T(8,128)S(1)}, f32[24,128]{1,0:T(8,128)S(1)}, u32[]{:S(2)}, u32[]{:S(2)}) collective-permute-start(f32[24,128]{1,0:T(8,128)S(1)} %get-tuple-element.26.s0_ref), channel_id=1, source_target_pairs={{0,2},{1,3},{2,0},{3,1},{4,6},{5,7},{6,4},{7,5},{8,10},{9,11},{10,... | collective-permute-start | bytes 36872 | tf_op jit(solution)/shard_map/ppermute | solution.py:303
  54.7 0.8 %collective-permute-start.3 = (f32[24,128]{1,0:T(8,128)S(1)}, f32[24,128]{1,0:T(8,128)S(1)}, u32[]{:S(2)}, u32[]{:S(2)}) collective-permute-start(f32[24,128]{1,0:T(8,128)S(1)} %get-tuple-element.26.s0_ref), channel_id=1, source_target_pairs={{0,1},{1,2},{2,3},{3,0},{4,5},{5,6},{6,7},{7,4},{8,9},{9,10},{10,1... | collective-permute-start | bytes 36872 | tf_op jit(solution)/shard_map/ppermute | solution.py:303
  55.5 0.3 collective-permute-done.5.s3_ref
  55.8 1.6 %collective-permute-done.4.s2_ref = f32[24,128]{1,0:T(8,128)S(1)} collective-permute-done((f32[24,128]{1,0:T(8,128)S(1)}, f32[24,128]{1,0:T(8,128)S(1)}, u32[]{:S(2)}, u32[]{:S(2)}) %collective-permute-start.4) | collective-permute-done | bytes 12320 | tf_op jit(solution)/shard_map/ppermute | solution.py:303
  57.4 1.3 %collective-permute-done.3.s1_ref = f32[24,128]{1,0:T(8,128)S(1)} collective-permute-done((f32[24,128]{1,0:T(8,128)S(1)}, f32[24,128]{1,0:T(8,128)S(1)}, u32[]{:S(2)}, u32[]{:S(2)}) %collective-permute-start.3) | collective-permute-done | bytes 12320 | tf_op jit(solution)/shard_map/ppermute | solution.py:303
  58.7 2.9 %normback.1 = (bf16[1536,640]{1,0:T(8,128)(2,1)}, bf16[1536,128]{1,0:T(8,128)(2,1)}) custom-call(bf16[1536,640]{1,0:T(8,128)(2,1)S(1)} %copy-done.1, bf16[1536,128]{1,0:T(8,128)(2,1)S(1)} %copy-done.3, bf16[1536,640]{1,0:T(8,128)(2,1)S(1)} %get-tuple-element.23.dq_ref, bf16[1536,128]{1,0:T(8,128)(2,1)S(1)} %get-tuple-element.24.dk_ref, ...), custom_call_target="tpu_custom_call" | custom-call | flops 10000000 | bytes 1000000 | tf_op jit(solution)/shard_map/normback/pallas_call | solution.py:349
  61.7 0.7 %assemble.1 = f32[5,3456]{1,0:T(8,128)} custom-call(f32[64,8,128]{2,1,0:T(8,128)S(1)} %all-to-all-done.got_ref, f32[8,384]{1,0:T(8,128)S(1)} %get-tuple-element.31.home_ref), custom_call_target="tpu_custom_call" | custom-call | flops 10000000 | bytes 1000000 | tf_op jit(solution)/shard_map/assemble/pallas_call | solution.py:352
  (23 shorter events, 0.0 us)
Async XLA Ops:
  0.6 1.5 %copy-start = (bf16[1536,640]{1,0:T(8,128)(2,1)S(1)}, bf16[1536,640]{1,0:T(8,128)(2,1)}, u32[]{:S(2)}) copy-start(bf16[1536,640]{1,0:T(8,128)(2,1)} %q_ref.7) | copy-start | bytes 5898244
  2.2 1.0 %copy-start.2 = (bf16[1536,128]{1,0:T(8,128)(2,1)S(1)}, bf16[1536,128]{1,0:T(8,128)(2,1)}, u32[]{:S(2)}) copy-start(bf16[1536,128]{1,0:T(8,128)(2,1)} %k_ref.7) | copy-start | bytes 1179652
  3.2 5.3 %copy-start.12 = (f32[640]{0:T(1024)S(1)}, f32[640]{0:T(1024)}, u32[]{:S(2)}) copy-start(f32[640]{0:T(1024)} %param.13) | copy-start | bytes 7684
  3.2 5.3 %copy-start.5 = (s32[1,36]{1,0:T(1,128)S(1)}, s32[1,36]{1,0:T(1,128)}, u32[]{:S(2)}) copy-start(s32[1,36]{1,0:T(1,128)} %len_ref.3) | copy-start | bytes 436
  3.2 8.4 %copy-start.1 = (bf16[1536,640]{1,0:T(8,128)(2,1)S(1)}, bf16[1536,640]{1,0:T(8,128)(2,1)}, u32[]{:S(2)}) copy-start(bf16[1536,640]{1,0:T(8,128)(2,1)} %q_ref.7) | copy-start | bytes 5898244
  3.2 8.4 %copy-start.3 = (bf16[1536,128]{1,0:T(8,128)(2,1)S(1)}, bf16[1536,128]{1,0:T(8,128)(2,1)}, u32[]{:S(2)}) copy-start(bf16[1536,128]{1,0:T(8,128)(2,1)} %k_ref.7) | copy-start | bytes 1179652
  3.2 8.4 %copy-start.4 = (f32[128]{0:T(128)S(1)}, f32[128]{0:T(128)}, u32[]{:S(2)}) copy-start(f32[128]{0:T(128)} %param.14) | copy-start | bytes 1540
  3.2 8.4 %copy-start.6 = (s32[1,36]{1,0:T(1,128)S(1)}, s32[1,36]{1,0:T(1,128)}, u32[]{:S(2)}) copy-start(s32[1,36]{1,0:T(1,128)} %dest_ref.1) | copy-start | bytes 436
  3.2 8.4 %copy-start.7 = (s32[1,36]{1,0:T(1,128)S(1)}, s32[1,36]{1,0:T(1,128)}, u32[]{:S(2)}) copy-start(s32[1,36]{1,0:T(1,128)} %shift_ref.1) | copy-start | bytes 436
  3.8 34.1 %copy-start.11 = (bf16[1536,128]{1,0:T(8,128)(2,1)S(1)}, bf16[1536,128]{1,0:T(8,128)(2,1)}, u32[]{:S(2)}) copy-start(bf16[1536,128]{1,0:T(8,128)(2,1)} %v_ref.1) | copy-start | bytes 1179652
  3.8 6.6 %collective-permute-start.2 = (f32[24,128]{1,0:T(8,128)S(1)}, f32[24,128]{1,0:T(8,128)S(1)}, u32[]{:S(2)}, u32[]{:S(2)}) collective-permute-start(f32[24,128]{1,0:T(8,128)S(1)} %squares.1.s0_ref), channel_id=1, source_target_pairs={{0,3},{1,0},{2,1},{3,2},{4,7},{5,4},{6,5},{7,6},{8,11},{9,8},{10,9... | collective-permute-start | bytes 36872 | tf_op jit(solution)/shard_map/ppermute | solution.py:303
  7.4 4.1 %collective-permute-start.1 = (f32[24,128]{1,0:T(8,128)S(1)}, f32[24,128]{1,0:T(8,128)S(1)}, u32[]{:S(2)}, u32[]{:S(2)}) collective-permute-start(f32[24,128]{1,0:T(8,128)S(1)} %squares.1.s0_ref), channel_id=1, source_target_pairs={{0,2},{1,3},{2,0},{3,1},{4,6},{5,7},{6,4},{7,5},{8,10},{9,11},{10,... | collective-permute-start | bytes 36872 | tf_op jit(solution)/shard_map/ppermute | solution.py:303
  7.8 3.8 %collective-permute-start = (f32[24,128]{1,0:T(8,128)S(1)}, f32[24,128]{1,0:T(8,128)S(1)}, u32[]{:S(2)}, u32[]{:S(2)}) collective-permute-start(f32[24,128]{1,0:T(8,128)S(1)} %squares.1.s0_ref), channel_id=1, source_target_pairs={{0,1},{1,2},{2,3},{3,0},{4,5},{5,6},{6,7},{7,4},{8,9},{9,10},{10,1... | collective-permute-start | bytes 36872 | tf_op jit(solution)/shard_map/ppermute | solution.py:303
  22.8 1.3 %copy-start.9 = (bf16[1536,640]{1,0:T(8,128)(2,1)}, bf16[1536,640]{1,0:T(8,128)(2,1)S(1)}, u32[]{:S(2)}) copy-start(bf16[1536,640]{1,0:T(8,128)(2,1)S(1)} %get-tuple-element.20.qn_ref) | copy-start | bytes 5898244
  24.1 37.6 %all-to-all-start = ((f32[64,8,128]{2,1,0:T(8,128)}), f32[64,8,128]{2,1,0:T(8,128)S(1)}, u32[]{:S(2)}, u32[]{:S(2)}) async-start(f32[64,8,128]{2,1,0:T(8,128)} %get-tuple-element.30), calls=%async_computation | async-start | bytes 524288 | tf_op jit(solution)/shard_map/all_to_all | solution.py:340
  37.9 1.5 %copy-start.8 = (bf16[1536,640]{1,0:T(8,128)(2,1)S(1)}, bf16[1536,640]{1,0:T(8,128)(2,1)}, u32[]{:S(2)}) copy-start(bf16[1536,640]{1,0:T(8,128)(2,1)} %g_ref.1) | copy-start | bytes 5898244
  39.4 1.5 %copy-start.10 = (bf16[1536,640]{1,0:T(8,128)(2,1)S(1)}, bf16[1536,640]{1,0:T(8,128)(2,1)}, u32[]{:S(2)}) copy-start(bf16[1536,640]{1,0:T(8,128)(2,1)} %copy-done.9) | copy-start | bytes 5898244
  53.2 2.5 %collective-permute-start.5 = (f32[24,128]{1,0:T(8,128)S(1)}, f32[24,128]{1,0:T(8,128)S(1)}, u32[]{:S(2)}, u32[]{:S(2)}) collective-permute-start(f32[24,128]{1,0:T(8,128)S(1)} %get-tuple-element.26.s0_ref), channel_id=1, source_target_pairs={{0,3},{1,0},{2,1},{3,2},{4,7},{5,4},{6,5},{7,6},{8,11},{9,8},{10,9... | collective-permute-start | bytes 36872 | tf_op jit(solution)/shard_map/ppermute | solution.py:303
  53.4 4.0 %collective-permute-start.4 = (f32[24,128]{1,0:T(8,128)S(1)}, f32[24,128]{1,0:T(8,128)S(1)}, u32[]{:S(2)}, u32[]{:S(2)}) collective-permute-start(f32[24,128]{1,0:T(8,128)S(1)} %get-tuple-element.26.s0_ref), channel_id=1, source_target_pairs={{0,2},{1,3},{2,0},{3,1},{4,6},{5,7},{6,4},{7,5},{8,10},{9,11},{10,... | collective-permute-start | bytes 36872 | tf_op jit(solution)/shard_map/ppermute | solution.py:303
  54.7 4.1 %collective-permute-start.3 = (f32[24,128]{1,0:T(8,128)S(1)}, f32[24,128]{1,0:T(8,128)S(1)}, u32[]{:S(2)}, u32[]{:S(2)}) collective-permute-start(f32[24,128]{1,0:T(8,128)S(1)} %get-tuple-element.26.s0_ref), channel_id=1, source_target_pairs={{0,1},{1,2},{2,3},{3,0},{4,5},{5,6},{6,7},{7,4},{8,9},{9,10},{10,1... | collective-permute-start | bytes 36872 | tf_op jit(solution)/shard_map/ppermute | solution.py:303

commit v2 on v1

v2 whole, which is shorter than its diff:
```python
import functools
import math

import jax
import jax.numpy as jnp
from jax import lax
from jax.experimental import pallas as pl
from jax.experimental.pallas import tpu as pltpu
from jax.sharding import PartitionSpec as P

HDIM = 128
TILE = 128
SEQ = 1536
TILES = SEQ // TILE
GROUP = 5
DOCS = 36
DEVICES = 64
SLOT = 48
HOME = 384
STAYING = 4
WINDOWS = (128, 160, 192, 256, 384, 512)
KEPT_ROWS = TILES * 192 + 576
FAR_ROWS = 40000
WIDTH_Q = 2560
WIDTH_K = 512

eps = 1e-06
big_negative = -1e30
scaling = 1.0 / math.sqrt(HDIM)
log2e = math.log2(math.e)
to_exp2 = scaling * log2e

f32 = jnp.float32
bf16 = jnp.bfloat16

VMEM = pl.BlockSpec(memory_space=pltpu.VMEM)
SMEM = pl.BlockSpec(memory_space=pltpu.SMEM)
HBM = pl.BlockSpec(memory_space=pltpu.HBM)

mxu_nt = functools.partial(
    lax.dot_general, dimension_numbers=(((1,), (1,)), ((), ())), preferred_element_type=f32
)
mxu_nn = functools.partial(
    lax.dot_general, dimension_numbers=(((1,), (0,)), ((), ())), preferred_element_type=f32
)
mxu_tn = functools.partial(
    lax.dot_general, dimension_numbers=(((0,), (0,)), ((), ())), preferred_element_type=f32
)


def call(kernel, outs, ins, out_specs=None, scratch=(), flops=10**7, vmem=8, name=None):
    shapes = [jax.ShapeDtypeStruct(s, d) for s, d in outs]
    return pl.pallas_call(
        kernel,
        out_shape=shapes,
        in_specs=ins,
        out_specs=out_specs or [VMEM] * len(outs),
        scratch_shapes=list(scratch),
        compiler_params=pltpu.CompilerParams(vmem_limit_bytes=int(vmem * 2**20)),
        cost_estimate=pl.CostEstimate(flops=flops, bytes_accessed=10**6, transcendentals=0),
        name=name,
    )


def row_sums(values):
    return jnp.sum(jnp.transpose(values), axis=0, keepdims=True)


def column(row):
    return jnp.transpose(jnp.broadcast_to(row, (TILE, TILE)))


def spread(values):
    return jnp.concatenate([values] * GROUP, axis=1)


def fold(values):
    total = values[:, :HDIM]
    for h in range(1, values.shape[1] // HDIM):
        total = total + values[:, h * HDIM : (h + 1) * HDIM]
    return total


def turned(rows):
    return jnp.transpose(jnp.concatenate([rows, jnp.zeros((TILE - 2 * TILES, TILE), f32)], axis=0))


CHUNKS = 4
CHUNK = SEQ // CHUNKS


def square_kernel(q_ref, k_ref, out_ref, q_buf, k_buf, sems):
    copies = []
    for c in range(CHUNKS):
        rows = pl.ds(c * CHUNK, CHUNK)
        copies.append(pltpu.make_async_copy(q_ref.at[rows], q_buf.at[rows], sems.at[c]))
    copies.append(pltpu.make_async_copy(k_ref, k_buf, sems.at[CHUNKS]))
    copies[CHUNKS].start()
    for copy in copies[:CHUNKS]:
        copy.start()
    copies[CHUNKS].wait()
    for i in range(TILES):
        k = k_buf[i * TILE : (i + 1) * TILE, :].astype(f32)
        out_ref[TILES + i : TILES + i + 1, :] = row_sums(k * k)
    for i in range(TILES):
        if i % (TILES // CHUNKS) == 0:
            copies[i // (TILES // CHUNKS)].wait()
        q = q_buf[i * TILE : (i + 1) * TILE, :].astype(f32)
        out_ref[i : i + 1, :] = row_sums(fold(q * q))


def layout_kernel(me_ref, len_ref, dest_ref, start_ref, tile_ref, doc_ref, stay_ref):
    rows = start_ref.shape[0]
    position = lax.broadcasted_iota(jnp.int32, (rows, TILE), 0) * TILE + lax.broadcasted_iota(
        jnp.int32, (rows, TILE), 1
    )
    zero = jnp.int32(0)
    me = me_ref[0]

    def step(j, carry):
        end, start, kept, count, lows = carry
        length = len_ref[0, j]
        stays = dest_ref[0, j] == me
        doc_ref[j] = end
        slot = jnp.where(stays, jnp.minimum(count, STAYING - 1), STAYING)
        stay_ref[slot] = end
        stay_ref[8 + slot] = kept
        stay_ref[16 + slot] = length
        kept = jnp.where(stays, kept + length, kept)
        count = jnp.where(stays, count + 1, count)
        end = end + length
        start = jnp.where(position >= end, end, start)
        lows = tuple(jnp.where(end <= i * TILE, end, low) for i, low in enumerate(lows))
        return end, start, kept, count, lows

    _, start, _, _, lows = lax.fori_loop(
        0,
        DOCS,
        step,
        (zero, jnp.zeros((rows, TILE), jnp.int32), zero, zero, (zero,) * TILES),
    )
    start_ref[...] = start
    base = zero
    for i in range(TILES):
        need = (i + 1) * TILE - lows[i]
        size = jnp.int32(WINDOWS[0])
        for smaller, larger in zip(WINDOWS, WINDOWS[1:]):
            size = jnp.where(need > smaller, larger, size)
        tile_ref[i] = (i + 1) * TILE - size
        tile_ref[16 + i] = size
        tile_ref[32 + i] = base
        base = base + size


def window_of(tile_ref, i, size):
    return pl.ds(pl.multiple_of(tile_ref[i], 32), size), pl.ds(
        pl.multiple_of(tile_ref[32 + i], 32), size
    )


def kept_at(tile_ref, i, size, part):
    return pl.ds(pl.multiple_of(part * KEPT_ROWS + tile_ref[32 + i], 32), size)


def for_size(tile_ref, i, body):
    size_here = tile_ref[16 + i]
    for size in WINDOWS:

        @pl.when(size_here == size)
        def _(size=size):
            body(size)


def stacked(ref, rows):
    return jnp.concatenate([ref[rows, h * HDIM : (h + 1) * HDIM] for h in range(GROUP)], axis=0)


def scores_kernel(
    tile_ref, start_ref, q_hbm, k_hbm, v_hbm, g_hbm, qg_ref, kg_ref, s0_ref, s1_ref, s2_ref, s3_ref,
    kn_ref, recip_ref, lse_ref, kept_ref, dots_ref,
    dot_acc, qn_ref, q_ref, g_ref, k_ref, v_ref, buf_ref, in_sems, thin_sems, qn_sems, sems,
):
    per_chunk = TILES // CHUNKS

    def arrival(which, c):
        far, near = ((q_hbm, q_ref), (g_hbm, g_ref))[which]
        part = pl.ds(pl.multiple_of(c * CHUNK, CHUNK), CHUNK)
        return pltpu.make_async_copy(far.at[part], near.at[part], in_sems.at[which, c])

    k_copy = pltpu.make_async_copy(k_hbm, k_ref, thin_sems.at[0])
    v_copy = pltpu.make_async_copy(v_hbm, v_ref, thin_sems.at[1])
    k_copy.start()
    for c in range(CHUNKS):
        arrival(0, c).start()
    v_copy.start()
    for c in range(CHUNKS):
        arrival(1, c).start()
    total = s0_ref[...] + s1_ref[...] + s2_ref[...] + s3_ref[...]
    recip = jnp.concatenate(
        [
            lax.rsqrt(total[:TILES] * (1.0 / WIDTH_Q) + eps),
            lax.rsqrt(total[TILES:] * (1.0 / WIDTH_K) + eps),
        ],
        axis=0,
    )
    recip_ref[...] = recip
    columns = turned(recip)
    lse_ref[TILES:] = jnp.zeros((lse_ref.shape[0] - TILES, 8, TILE), f32)
    dot_acc[...] = jnp.zeros(dot_acc.shape, f32)
    k_copy.wait()
    for i in range(TILES):
        rows = slice(i * TILE, (i + 1) * TILE)
        col_k = columns[:, TILES + i : TILES + i + 1]
        kn_ref[rows, :] = (k_ref[rows, :].astype(f32) * col_k * kg_ref[...]).astype(bf16)

    def departure(c):
        near = pl.ds(pl.multiple_of(c * CHUNK, CHUNK), CHUNK)
        far = pl.ds(pl.multiple_of(2 * KEPT_ROWS + c * CHUNK, 32), CHUNK)
        return pltpu.make_async_copy(qn_ref.at[near], kept_ref.at[far], qn_sems.at[c])

    for i in range(TILES):
        if i % per_chunk == 0:
            arrival(0, i // per_chunk).wait()
        rows = slice(i * TILE, (i + 1) * TILE)
        col_q = columns[:, i : i + 1]
        qn_ref[rows, :] = (q_ref[rows, :].astype(f32) * col_q * qg_ref[...]).astype(bf16)
        if (i + 1) % per_chunk == 0:
            departure(i // per_chunk).start()
    v_copy.wait()

    def copies(i, size):
        return [
            pltpu.make_async_copy(
                buf_ref.at[kept_at(tile_ref, i, size, part)],
                kept_ref.at[kept_at(tile_ref, i, size, part)],
                sems.at[part, i],
            )
            for part in range(2)
        ]

    def tile_step(i, carry):
        rows = pl.ds(pl.multiple_of(i * TILE, TILE), TILE)
        start_row = start_ref[pl.ds(i, 1), :]

        @pl.when(lax.rem(i, per_chunk) == 0)
        def _():
            arrival(1, lax.div(i, per_chunk)).wait()

        def body(size):
            window = pl.ds(pl.multiple_of(tile_ref[i], 32), size)
            keys = kn_ref[window, :]
            values = v_ref[window, :]
            key = tile_ref[i] + lax.broadcasted_iota(jnp.int32, (size, TILE), 0)
            query = i * TILE + lax.broadcasted_iota(jnp.int32, (size, TILE), 1)
            bias = jnp.where((key >= start_row) & (key <= query), 0.0, big_negative)
            qs = stacked(qn_ref, rows)
            gs = stacked(g_ref, rows)
            masked = mxu_nt(keys, qs) + spread(bias)
            grad_weights = mxu_nt(values, gs)
            peak = jnp.max(masked, axis=0, keepdims=True)
            grown = jnp.exp2(masked * to_exp2 - peak * to_exp2)
            mass = jnp.sum(grown, axis=0, keepdims=True)
            logs = peak * scaling + jnp.log(mass)
            inverse = 1.0 / mass
            low = (grown * inverse).astype(bf16)
            buf_ref[kept_at(tile_ref, i, size, 0), :] = low
            delta = jnp.sum(low.astype(f32) * grad_weights, axis=0, keepdims=True)
            grad = grown * (inverse * scaling) * (grad_weights - delta)
            buf_ref[kept_at(tile_ref, i, size, 1), :] = grad.astype(bf16)
            dots = fold(grad * masked)
            logs = [logs[:, h * HDIM : (h + 1) * HDIM] for h in range(GROUP)]
            logs.append(jnp.zeros((8 - GROUP, TILE), f32))
            lse_ref[pl.ds(i, 1)] = jnp.concatenate(logs, axis=0)[None]
            dots_ref[pl.ds(i, 1), :] = jnp.sum(dots, axis=0, keepdims=True)
            dot_acc[window, :] += dots
            for copy in copies(i, size):
                copy.start()

        for_size(tile_ref, i, body)
        return carry

    lax.fori_loop(0, TILES, tile_step, 0)
    for i in range(TILES):
        dots_ref[TILES + i : TILES + i + 1, :] = row_sums(dot_acc[i * TILE : (i + 1) * TILE, :])
    for c in range(CHUNKS):
        departure(c).wait()

    def drain(i, carry):
        def body(size):
            for copy in copies(i, size):
                copy.wait()

        for_size(tile_ref, i, body)
        return carry

    lax.fori_loop(0, TILES, drain, 0)


def slot_kernel(
    me_ref, doc_ref, stay_ref, len_ref, dest_ref, shift_ref, lse_ref, slot_ref, home_ref, work
):
    me = me_ref[0]
    lane = lax.broadcasted_iota(jnp.int32, (8, TILE), 1)
    work[...] = jnp.zeros(work.shape, f32)
    for j in range(DOCS):
        dest = dest_ref[0, j]
        length = jnp.where(dest == me, 0, len_ref[0, j])
        block = doc_ref[j] >> 7
        inner = doc_ref[j] & (TILE - 1)
        place = shift_ref[0, j]
        turn = (place - inner) & (TILE - 1)
        here = pltpu.roll(lse_ref[block], turn, 1)
        after = pltpu.roll(lse_ref[block + 1], turn, 1)
        index = lane - place
        value = jnp.where(index < TILE - inner, here, after)
        work[dest] = jnp.where((index >= 0) & (index < length), value, 0.0)
    heads = [work[:, h, :] for h in range(GROUP)]
    wide = lax.broadcasted_iota(jnp.int32, (DEVICES, TILE), 1)
    gap_low = (wide >= 48) & (wide < 64)
    gap_high = wide >= 112
    last = heads[4]
    slot_ref[:, 0, :] = jnp.where(
        gap_low,
        pltpu.roll(last, 48, 1),
        jnp.where(gap_high, pltpu.roll(last, 96, 1), heads[0] + pltpu.roll(heads[1], 64, 1)),
    )
    slot_ref[:, 1, :] = jnp.where(
        gap_low, pltpu.roll(last, 16, 1), heads[2] + pltpu.roll(heads[3], 64, 1)
    )
    homes = [jnp.zeros((8, TILE), f32)] * (HOME // TILE)
    for n in range(STAYING):
        kept = stay_ref[8 + n]
        length = stay_ref[16 + n]
        gap = stay_ref[n] - kept
        block = gap >> 7
        inner = gap & (TILE - 1)
        turn = (TILE - inner) & (TILE - 1)
        moved = [pltpu.roll(lse_ref[block + b], turn, 1) for b in range(HOME // TILE + 1)]
        for b in range(HOME // TILE):
            value = jnp.where(lane < TILE - inner, moved[b], moved[b + 1])
            column = lane + b * TILE
            inside = (column >= kept) & (column < kept + length)
            homes[b] = jnp.where(inside, value, homes[b])
    home_ref[...] = jnp.concatenate(homes, axis=1)


def finish_kernel(
    tile_ref, kn_hbm, kept_ref, g_hbm, q_hbm, k_hbm, qg_ref, kg_ref, recip_ref,
    s0_ref, s1_ref, s2_ref, s3_ref,
    gq_ref, gk_ref, gv_ref,
    dk_acc, dv_acc, dq_buf, gq_buf, kn_ref, qn_ref, g_ref, q_ref, k_ref, gk_buf, gv_buf, buf_ref, cube_ref,
    in_sems, thin_sems, sems, out_sems,
):
    per_chunk = TILES // CHUNKS

    def chunk_copies(c):
        part = pl.ds(pl.multiple_of(c * CHUNK, CHUNK), CHUNK)
        far = pl.ds(pl.multiple_of(2 * KEPT_ROWS + c * CHUNK, 32), CHUNK)
        return [
            pltpu.make_async_copy(kept_ref.at[far], qn_ref.at[part], in_sems.at[0, c]),
            pltpu.make_async_copy(g_hbm.at[part], g_ref.at[part], in_sems.at[1, c]),
            pltpu.make_async_copy(q_hbm.at[part], q_ref.at[part], in_sems.at[2, c]),
        ]

    def out_copy(c):
        part = pl.ds(pl.multiple_of(c * CHUNK, CHUNK), CHUNK)
        return pltpu.make_async_copy(gq_buf.at[part], gq_ref.at[part], out_sems.at[c])

    def copies(i, size):
        return [
            pltpu.make_async_copy(
                kept_ref.at[kept_at(tile_ref, i, size, part)],
                buf_ref.at[kept_at(tile_ref, i, size, part)],
                sems.at[part, i],
            )
            for part in range(2)
        ]

    kn_copy = pltpu.make_async_copy(kn_hbm, kn_ref, thin_sems.at[0])
    k_copy = pltpu.make_async_copy(k_hbm, k_ref, thin_sems.at[1])
    gk_copy = pltpu.make_async_copy(gk_buf, gk_ref, thin_sems.at[2])
    gv_copy = pltpu.make_async_copy(gv_buf, gv_ref, thin_sems.at[3])
    kn_copy.start()

    def begin(i, carry):
        @pl.when(lax.rem(i, per_chunk) == 0)
        def _():
            for copy in chunk_copies(lax.div(i, per_chunk)):
                copy.start()

        def body(size):
            for copy in copies(i, size):
                copy.start()

        for_size(tile_ref, i, body)
        return carry

    lax.fori_loop(0, TILES, begin, 0)
    k_copy.start()
    dk_acc[...] = jnp.zeros(dk_acc.shape, f32)
    dv_acc[...] = jnp.zeros(dv_acc.shape, f32)
    recip = recip_ref[...]
    dots = s0_ref[...] + s1_ref[...] + s2_ref[...] + s3_ref[...]
    cube_ref[:TILES, :] = recip[:TILES] * recip[:TILES] * dots[:TILES] * (1.0 / WIDTH_Q)
    cube_ref[TILES:, :] = recip[TILES:] * recip[TILES:] * dots[TILES:] * (1.0 / WIDTH_K)
    kn_copy.wait()

    def finish_queries(i):
        rows = pl.ds(pl.multiple_of(i * TILE, TILE), TILE)
        factor = spread(column(recip_ref[pl.ds(i, 1), :])) * qg_ref[...]
        cube = spread(column(cube_ref[pl.ds(i, 1), :]))
        gq_buf[rows, :] = (
            factor * dq_buf[rows, :].astype(f32) - q_ref[rows, :].astype(f32) * cube
        ).astype(bf16)

    def tile_step(i, carry):
        rows = pl.ds(pl.multiple_of(i * TILE, TILE), TILE)

        @pl.when(lax.rem(i, per_chunk) == 0)
        def _():
            for copy in chunk_copies(lax.div(i, per_chunk)):
                copy.wait()

        def body(size):
            for copy in copies(i, size):
                copy.wait()
            finish_queries(jnp.maximum(i - 1, 0))
            window = pl.ds(pl.multiple_of(tile_ref[i], 32), size)
            weights = buf_ref[kept_at(tile_ref, i, size, 0), :]
            grads = buf_ref[kept_at(tile_ref, i, size, 1), :]
            dv_acc[window, :] += mxu_nn(weights, stacked(g_ref, rows))
            dk_acc[window, :] += mxu_nn(grads, stacked(qn_ref, rows))
            dq = mxu_tn(grads, kn_ref[window, :]).astype(bf16)
            for h in range(GROUP):
                dq_buf[rows, h * HDIM : (h + 1) * HDIM] = dq[h * TILE : (h + 1) * TILE]

        for_size(tile_ref, i, body)

        @pl.when((lax.rem(i, per_chunk) == 0) & (i > 0))
        def _():
            out_copy(lax.div(i, per_chunk) - 1).start()

        return carry

    dq_buf[:TILE, :] = jnp.zeros((TILE, GROUP * HDIM), bf16)
    lax.fori_loop(0, TILES, tile_step, 0)
    finish_queries(TILES - 1)
    out_copy(CHUNKS - 1).start()
    gv_buf[...] = dv_acc[...].astype(bf16)
    gv_copy.start()
    k_copy.wait()
    for i in range(TILES):
        rows = slice(i * TILE, (i + 1) * TILE)
        at = slice(TILES + i, TILES + i + 1)
        scaled = dk_acc[rows, :].astype(bf16).astype(f32) * kg_ref[...]
        gk_buf[rows, :] = (
            column(recip_ref[at, :]) * scaled - k_ref[rows, :].astype(f32) * column(cube_ref[at, :])
        ).astype(bf16)
    gk_copy.start()
    for c in range(CHUNKS):
        out_copy(c).wait()
    gv_copy.wait()
    gk_copy.wait()


def assemble_kernel(got_ref, home_ref, out_ref, work):
    out_ref[:, :HOME] = home_ref[:GROUP, :]
    upper, lower = got_ref[:, 0, :], got_ref[:, 1, :]
    wide = lax.broadcasted_iota(jnp.int32, (DEVICES, TILE), 1)
    work[:, 0, :] = upper
    work[:, 1, :] = pltpu.roll(upper, 64, 1)
    work[:, 2, :] = lower
    work[:, 3, :] = pltpu.roll(lower, 64, 1)
    work[:, 4, :] = jnp.where(
        wide < 16,
        pltpu.roll(upper, TILE - 48, 1),
        jnp.where(wide < 32, pltpu.roll(upper, TILE - 96, 1), pltpu.roll(lower, TILE - 16, 1)),
    )
    lane = lax.broadcasted_iota(jnp.int32, (8, TILE), 1)
    blocks = [None] * (DEVICES * SLOT // TILE)
    for s in range(DEVICES):
        block, place = divmod(s * SLOT, TILE)
        value = work[s]
        value = pltpu.roll(value, place, 1) if place else value
        if blocks[block] is None:
            blocks[block] = value
        else:
            blocks[block] = jnp.where(lane >= place, value, blocks[block])
        if place + SLOT > TILE:
            blocks[block + 1] = value
    for b, value in enumerate(blocks):
        out_ref[:, HOME + b * TILE : HOME + (b + 1) * TILE] = value[:GROUP]


def from_others(values):
    size = lax.axis_size("head")
    return [values] + [
        lax.ppermute(values, "head", [(i, (i + s) % size) for i in range(size)])
        for s in range(1, size)
    ]


def local(q_raw, k_raw, v_proj, d_out, q_gain, k_gain, doc_lengths, plan_dest, plan_offset):
    me = lax.axis_index("dp").astype(jnp.int32).reshape(1)
    qg = q_gain.reshape(1, -1)
    kg = k_gain.reshape(1, -1)
    stat = ((2 * TILES, TILE), f32)
    wide = ((SEQ, GROUP * HDIM), bf16)
    thin = ((SEQ, HDIM), bf16)
    logs = ((16, 8, TILE), f32)
    kept = ((FAR_ROWS, GROUP * HDIM), bf16)

    (squares,) = call(
        square_kernel,
        [stat],
        [HBM] * 2,
        scratch=[pltpu.VMEM(*wide), pltpu.VMEM(*thin), pltpu.SemaphoreType.DMA((CHUNKS + 1,))],
        vmem=53.7,
        name="squares",
    )(q_raw, k_raw)
    start, tiles, docs, stays = call(
        layout_kernel,
        [((16, TILE), jnp.int32), ((48,), jnp.int32), ((DOCS,), jnp.int32), ((24,), jnp.int32)],
        [SMEM] * 3,
        [VMEM] + [SMEM] * 3,
        name="layout",
    )(me, doc_lengths, plan_dest)
    kn, recip, lse, kept, dots = call(
        scores_kernel,
        [thin, stat, logs, kept, stat],
        [SMEM, VMEM] + [HBM] * 4 + [VMEM] * 6,
        out_specs=[VMEM] * 3 + [HBM, VMEM],
        scratch=[
            pltpu.VMEM((SEQ, HDIM), f32),
            pltpu.VMEM(*wide),
            pltpu.VMEM(*wide),
            pltpu.VMEM(*wide),
            pltpu.VMEM(*thin),
            pltpu.VMEM(*thin),
            pltpu.VMEM((2 * KEPT_ROWS, GROUP * HDIM), bf16),
            pltpu.SemaphoreType.DMA((2, CHUNKS)),
            pltpu.SemaphoreType.DMA((2,)),
            pltpu.SemaphoreType.DMA((CHUNKS,)),
            pltpu.SemaphoreType.DMA((2, TILES)),
        ],
        flops=10**9,
        vmem=53.7,
        name="scores",
    )(tiles, start, q_raw, k_raw, v_proj, d_out, qg, kg, *from_others(squares))
    all_dots = from_others(dots)
    slots, home = call(
        slot_kernel,
        [((DEVICES, 2, TILE), f32), ((8, HOME), f32)],
        [SMEM] * 6 + [VMEM],
        scratch=[pltpu.VMEM((DEVICES, 8, TILE), f32)],
        name="slots",
    )(me, docs, stays, doc_lengths, plan_dest, plan_offset, lse)
    got = lax.all_to_all(slots, "dp", split_axis=0, concat_axis=0, tiled=True)
    grad_q, grad_k, grad_v = call(
        finish_kernel,
        [wide, thin, thin],
        [SMEM] + [HBM] * 5 + [VMEM] * 7,
        out_specs=[HBM] * 3,
        scratch=[
            pltpu.VMEM((SEQ, HDIM), f32),
            pltpu.VMEM((SEQ, HDIM), f32),
            pltpu.VMEM(*wide),
            pltpu.VMEM(*wide),
            pltpu.VMEM(*thin),
            pltpu.VMEM(*wide),
            pltpu.VMEM(*wide),
            pltpu.VMEM(*wide),
            pltpu.VMEM(*thin),
            pltpu.VMEM(*thin),
            pltpu.VMEM(*thin),
            pltpu.VMEM((2 * KEPT_ROWS, GROUP * HDIM), bf16),
            pltpu.VMEM((2 * TILES, TILE), f32),
            pltpu.SemaphoreType.DMA((3, CHUNKS)),
            pltpu.SemaphoreType.DMA((4,)),
            pltpu.SemaphoreType.DMA((2, TILES)),
            pltpu.SemaphoreType.DMA((CHUNKS,)),
        ],
        flops=10**10,
        vmem=53.7,
        name="finish",
    )(tiles, kn, kept, d_out, q_raw, k_raw, qg, kg, recip, *all_dots)
    (balanced,) = call(
        assemble_kernel,
        [((GROUP, HOME + DEVICES * SLOT), f32)],
        [VMEM] * 2,
        scratch=[pltpu.VMEM((DEVICES, 8, TILE), f32)],
        name="assemble",
    )(got, home)
    return grad_q, grad_k, grad_v, balanced


def solution(mesh):
    in_specs = (
        P("dp", "head"),
        P("dp", "head"),
        P("dp", "head"),
        P("dp", "head"),
        P("head"),
        P("head"),
        P("dp", None),
        P("dp", None),
        P("dp", None),
    )
    out_specs = (P("dp", "head"), P("dp", "head"), P("dp", "head"), P("head", "dp"))
    return jax.shard_map(local, mesh=mesh, in_specs=in_specs, out_specs=out_specs, check_vma=False)
```

time: 63.3 us -> 52.3 us (0.83)
  local copies, waits for them, and re-layouts: 6.92 us -> 0.02 us
  waiting for transfers between devices: 4.42 us -> 1.82 us
    unnamed x26 -> x10, local copies, waits for them, and re-layouts: 6.92 us -> 0.02 us
    ppermute x6, waiting for transfers between devices: 4.42 us -> 0.89 us  [from_others(): lax.ppermute(values, 'head', [(i, (i + s) % size) for i in range(size)])]
    all_to_all x1, starting transfers between devices: 13.8 us -> 12.8 us  [local(): got = lax.all_to_all(slots, 'dp', split_axis=0, concat_axis=0, tiled=True)]
    all_to_all x1, waiting for transfers between devices: 0.01 us -> 0.93 us  [local(): got = lax.all_to_all(slots, 'dp', split_axis=0, concat_axis=0, tiled=True)]
    pallas_call x5, Pallas kernels: 28.8 us -> 28 us  [the longest x1 13.1 us: local(): call(scores_kernel, [thin, stat, logs, kept, stat], [SMEM, VMEM] + [HBM]...]
  transfers between devices with their start and end apart: 7 -> 7, of which waited for: 5 -> 3; matrix products, arithmetic and copies ran while one was open for 0% -> 0% of each run, Pallas kernels for 27% -> 25%
where the time goes in v2:
time: 52.3 us; the launch traced here: 51.7 us
  Pallas kernels  29 us (55%)
  starting transfers between devices  20.2 us (39%)
  waiting for transfers between devices  1.82 us (3%)
  between operations  0.75 us (1%)
    pallas_call x1, Pallas kernels, local(): call(scores_kernel, [thin, stat, logs, kept, stat], [SMEM, VMEM] + [HBM]...  13.1 us
    all_to_all x1, starting transfers between devices, local(): got = lax.all_to_all(slots, 'dp', split_axis=0, concat_axis=0, tiled=True)  12.8 us
    pallas_call x1, Pallas kernels, local(): call(finish_kernel, [wide, thin, thin], [SMEM] + [HBM] * 5 + [VMEM] * 7,...  9.12 us
    ppermute x6, starting transfers between devices, from_others(): lax.ppermute(values, 'head', [(i, (i + s) % size) for i in range(size)])  7.32 us
    pallas_call x1, Pallas kernels, local(): call(layout_kernel, [((16, TILE), jnp.int32), ((48,), jnp.int32), ((DOCS,...  2.22 us
    pallas_call x1, Pallas kernels, local(): call(square_kernel, [stat], [HBM] * 2, scratch=[pltpu.VMEM(*wide), pltpu....  2.03 us
    pallas_call x1, Pallas kernels, local(): call(slot_kernel, [((DEVICES, 2, TILE), f32), ((8, HOME), f32)], [SMEM] *...  1.52 us
  transfers between devices with their start and end apart: 7, of which 3 were waited for; matrix products, arithmetic and copies ran while one was open for 0% of the time, Pallas kernels for 25%

profile of v2, /device:TPU:1, one launch (start us, length us, event | category | flops | bytes accessed | tf_op | source)
XLA Modules:
  0.0 51.7 jit_solution(6547621617370447990)
XLA Ops:
  0.6 0.0 copy-start.4
  0.6 0.0 copy-start.2
  0.7 2.0 %squares.1.s0_ref = f32[24,128]{1,0:T(8,128)S(1)} custom-call(bf16[1536,640]{1,0:T(8,128)(2,1)} %q_hbm.3, bf16[1536,128]{1,0:T(8,128)(2,1)} %k_hbm.3), custom_call_target="tpu_custom_call" | custom-call | flops 10000000 | bytes 1000000 | tf_op jit(solution)/shard_map/squares/pallas_call | solution.py:513
  2.7 3.6 %collective-permute-start.2 = (f32[24,128]{1,0:T(8,128)S(1)}, f32[24,128]{1,0:T(8,128)S(1)}, u32[]{:S(2)}, u32[]{:S(2)}) collective-permute-start(f32[24,128]{1,0:T(8,128)S(1)} %squares.1.s0_ref), channel_id=1, source_target_pairs={{0,3},{1,0},{2,1},{3,2},{4,7},{5,4},{6,5},{7,6},{8,11},{9,8},{10,9... | collective-permute-start | bytes 36872 | tf_op jit(solution)/shard_map/ppermute | solution.py:498
  6.3 0.3 collective-permute-start.1
  6.7 0.7 %collective-permute-start = (f32[24,128]{1,0:T(8,128)S(1)}, f32[24,128]{1,0:T(8,128)S(1)}, u32[]{:S(2)}, u32[]{:S(2)}) collective-permute-start(f32[24,128]{1,0:T(8,128)S(1)} %squares.1.s0_ref), channel_id=1, source_target_pairs={{0,1},{1,2},{2,3},{3,0},{4,5},{5,6},{6,7},{7,4},{8,9},{9,10},{10,1... | collective-permute-start | bytes 36872 | tf_op jit(solution)/shard_map/ppermute | solution.py:498
  7.4 0.0 copy-done.4
  7.4 2.2 %layout.1 = (s32[16,128]{1,0:T(8,128)S(1)}, s32[48]{0:T(128)S(1)}, s32[36]{0:T(128)S(1)}, s32[24]{0:T(128)S(1)}) custom-call(s32[1]{0:T(128)} %bitcast.me_ref, s32[1,36]{1,0:T(1,128)S(1)} %copy-done.1, s32[1,36]{1,0:T(1,128)S(1)} %copy-done.2), custom_call_target="tpu_custom_call" | custom-call | flops 10000000 | bytes 1000000 | tf_op jit(solution)/shard_map/layout/pallas_call | solution.py:521
  9.6 0.0 collective-permute-done.2.s3_ref
  9.6 0.8 %collective-permute-done.1.s2_ref = f32[24,128]{1,0:T(8,128)S(1)} collective-permute-done((f32[24,128]{1,0:T(8,128)S(1)}, f32[24,128]{1,0:T(8,128)S(1)}, u32[]{:S(2)}, u32[]{:S(2)}) %collective-permute-start.1) | collective-permute-done | bytes 12320 | tf_op jit(solution)/shard_map/ppermute | solution.py:498
  10.4 0.1 collective-permute-done.s1_ref
  10.5 13.1 %scores.1 = (bf16[1536,128]{1,0:T(8,128)(2,1)}, f32[24,128]{1,0:T(8,128)S(1)}, f32[16,8,128]{2,1,0:T(8,128)S(1)}, bf16[40000,640]{1,0:T(8,128)(2,1)}, f32[24,128]{1,0:T(8,128)S(1)}) custom-call(s32[48]{0:T(128)S(1)} %get-tuple-element.18.tile_ref, s32[16,128]{1,0:T(8,128)S(1)} %get-tuple-element.19.start_ref, bf16[1536,640]{1,0:T(8,128)(2,1)} %q_hbm.3, ...), custom_call_target="tpu_custom_call" | custom-call | flops 1000000000 | bytes 1000000 | tf_op jit(solution)/shard_map/scores/pallas_call | solution.py:528
  23.7 1.2 %collective-permute-start.5 = (f32[24,128]{1,0:T(8,128)S(1)}, f32[24,128]{1,0:T(8,128)S(1)}, u32[]{:S(2)}, u32[]{:S(2)}) collective-permute-start(f32[24,128]{1,0:T(8,128)S(1)} %get-tuple-element.23.s0_ref), channel_id=1, source_target_pairs={{0,3},{1,0},{2,1},{3,2},{4,7},{5,4},{6,5},{7,6},{8,11},{9,8},{10,9... | collective-permute-start | bytes 36872 | tf_op jit(solution)/shard_map/ppermute | solution.py:498
  24.9 1.4 %collective-permute-start.4 = (f32[24,128]{1,0:T(8,128)S(1)}, f32[24,128]{1,0:T(8,128)S(1)}, u32[]{:S(2)}, u32[]{:S(2)}) collective-permute-start(f32[24,128]{1,0:T(8,128)S(1)} %get-tuple-element.23.s0_ref), channel_id=1, source_target_pairs={{0,2},{1,3},{2,0},{3,1},{4,6},{5,7},{6,4},{7,5},{8,10},{9,11},{10,... | collective-permute-start | bytes 36872 | tf_op jit(solution)/shard_map/ppermute | solution.py:498
  26.3 0.0 collective-permute-start.3
  26.3 0.0 copy-done.3
  26.3 1.5 %slots.1 = (f32[64,2,128]{2,1,0:T(2,128)}, f32[8,384]{1,0:T(8,128)S(1)}) custom-call(s32[1]{0:T(128)} %bitcast.me_ref, s32[36]{0:T(128)S(1)} %get-tuple-element.27.doc_ref, s32[24]{0:T(128)S(1)} %get-tuple-element.28.stay_ref, s32[1,36]{1,0:T(1,128)S(1)} %copy-done.1, s32[1,36]{1,0:T(1,128)S(1)} %copy-done.2, s32[1,36]{1,0:T(1,128)S(1)} %copy-done.3, ...), custom_call_target="tpu_custom_call" | custom-call | flops 10000000 | bytes 1000000 | tf_op jit(solution)/shard_map/slots/pallas_call | solution.py:551
  27.8 12.8 %all-to-all-start = ((f32[64,2,128]{2,1,0:T(2,128)}), f32[64,2,128]{2,1,0:T(2,128)S(1)}, u32[]{:S(2)}, u32[]{:S(2)}) async-start(f32[64,2,128]{2,1,0:T(2,128)} %get-tuple-element.30), calls=%async_computation | async-start | bytes 131072 | tf_op jit(solution)/shard_map/all_to_all | solution.py:558
  40.7 0.0 collective-permute-done.5.s3_ref
  40.7 0.0 collective-permute-done.4.s2_ref
  40.7 0.0 collective-permute-done.3.s1_ref
  40.7 9.1 %finish.1 = (bf16[1536,640]{1,0:T(8,128)(2,1)}, bf16[1536,128]{1,0:T(8,128)(2,1)}, bf16[1536,128]{1,0:T(8,128)(2,1)}) custom-call(s32[48]{0:T(128)S(1)} %get-tuple-element.18.tile_ref, bf16[1536,128]{1,0:T(8,128)(2,1)} %get-tuple-element.20.kn_hbm, bf16[40000,640]{1,0:T(8,128)(2,1)} %get-tuple-element.21.kept_ref, bf16[1536,640]{1,0:T(8,128)(2,1)} %g_hbm.3, ...), custom_call_target="tpu_custom_call" | custom-call | flops 10000000000 | bytes 1000000 | tf_op jit(solution)/shard_map/finish/pallas_call | solution.py:559
  49.9 0.9 %all-to-all-done.got_ref = f32[64,2,128]{2,1,0:T(2,128)S(1)} async-done(((f32[64,2,128]{2,1,0:T(2,128)}), f32[64,2,128]{2,1,0:T(2,128)S(1)}, u32[]{:S(2)}, u32[]{:S(2)}) %all-to-all-start) | async-done | bytes 65568 | tf_op jit(solution)/shard_map/all_to_all | solution.py:558
  50.8 0.9 %assemble.1 = f32[5,3456]{1,0:T(8,128)} custom-call(f32[64,2,128]{2,1,0:T(2,128)S(1)} %all-to-all-done.got_ref, f32[8,384]{1,0:T(8,128)S(1)} %get-tuple-element.31.home_ref), custom_call_target="tpu_custom_call" | custom-call | flops 10000000 | bytes 1000000 | tf_op jit(solution)/shard_map/assemble/pallas_call | solution.py:587
  (7 shorter events, 0.0 us)
Async XLA Ops:
  0.6 6.8 %copy-start.4 = (f32[640]{0:T(1024)S(1)}, f32[640]{0:T(1024)}, u32[]{:S(2)}) copy-start(f32[640]{0:T(1024)} %param.13) | copy-start | bytes 7684
  0.6 6.8 %copy-start.2 = (s32[1,36]{1,0:T(1,128)S(1)}, s32[1,36]{1,0:T(1,128)}, u32[]{:S(2)}) copy-start(s32[1,36]{1,0:T(1,128)} %dest_ref.3) | copy-start | bytes 436
  0.7 6.8 %copy-start.1 = (s32[1,36]{1,0:T(1,128)S(1)}, s32[1,36]{1,0:T(1,128)}, u32[]{:S(2)}) copy-start(s32[1,36]{1,0:T(1,128)} %len_ref.3) | copy-start | bytes 436
  0.7 9.9 %copy-start = (f32[128]{0:T(128)S(1)}, f32[128]{0:T(128)}, u32[]{:S(2)}) copy-start(f32[128]{0:T(128)} %param.14) | copy-start | bytes 1540
  2.7 6.9 %collective-permute-start.2 = (f32[24,128]{1,0:T(8,128)S(1)}, f32[24,128]{1,0:T(8,128)S(1)}, u32[]{:S(2)}, u32[]{:S(2)}) collective-permute-start(f32[24,128]{1,0:T(8,128)S(1)} %squares.1.s0_ref), channel_id=1, source_target_pairs={{0,3},{1,0},{2,1},{3,2},{4,7},{5,4},{6,5},{7,6},{8,11},{9,8},{10,9... | collective-permute-start | bytes 36872 | tf_op jit(solution)/shard_map/ppermute | solution.py:498
  6.3 4.1 %collective-permute-start.1 = (f32[24,128]{1,0:T(8,128)S(1)}, f32[24,128]{1,0:T(8,128)S(1)}, u32[]{:S(2)}, u32[]{:S(2)}) collective-permute-start(f32[24,128]{1,0:T(8,128)S(1)} %squares.1.s0_ref), channel_id=1, source_target_pairs={{0,2},{1,3},{2,0},{3,1},{4,6},{5,7},{6,4},{7,5},{8,10},{9,11},{10,... | collective-permute-start | bytes 36872 | tf_op jit(solution)/shard_map/ppermute | solution.py:498
  6.7 3.8 %collective-permute-start = (f32[24,128]{1,0:T(8,128)S(1)}, f32[24,128]{1,0:T(8,128)S(1)}, u32[]{:S(2)}, u32[]{:S(2)}) collective-permute-start(f32[24,128]{1,0:T(8,128)S(1)} %squares.1.s0_ref), channel_id=1, source_target_pairs={{0,1},{1,2},{2,3},{3,0},{4,5},{5,6},{6,7},{7,4},{8,9},{9,10},{10,1... | collective-permute-start | bytes 36872 | tf_op jit(solution)/shard_map/ppermute | solution.py:498
  10.5 15.8 %copy-start.3 = (s32[1,36]{1,0:T(1,128)S(1)}, s32[1,36]{1,0:T(1,128)}, u32[]{:S(2)}) copy-start(s32[1,36]{1,0:T(1,128)} %shift_ref.1) | copy-start | bytes 436
  23.7 17.0 %collective-permute-start.5 = (f32[24,128]{1,0:T(8,128)S(1)}, f32[24,128]{1,0:T(8,128)S(1)}, u32[]{:S(2)}, u32[]{:S(2)}) collective-permute-start(f32[24,128]{1,0:T(8,128)S(1)} %get-tuple-element.23.s0_ref), channel_id=1, source_target_pairs={{0,3},{1,0},{2,1},{3,2},{4,7},{5,4},{6,5},{7,6},{8,11},{9,8},{10,9... | collective-permute-start | bytes 36872 | tf_op jit(solution)/shard_map/ppermute | solution.py:498
  24.9 15.8 %collective-permute-start.4 = (f32[24,128]{1,0:T(8,128)S(1)}, f32[24,128]{1,0:T(8,128)S(1)}, u32[]{:S(2)}, u32[]{:S(2)}) collective-permute-start(f32[24,128]{1,0:T(8,128)S(1)} %get-tuple-element.23.s0_ref), channel_id=1, source_target_pairs={{0,2},{1,3},{2,0},{3,1},{4,6},{5,7},{6,4},{7,5},{8,10},{9,11},{10,... | collective-permute-start | bytes 36872 | tf_op jit(solution)/shard_map/ppermute | solution.py:498
  26.3 14.4 %collective-permute-start.3 = (f32[24,128]{1,0:T(8,128)S(1)}, f32[24,128]{1,0:T(8,128)S(1)}, u32[]{:S(2)}, u32[]{:S(2)}) collective-permute-start(f32[24,128]{1,0:T(8,128)S(1)} %get-tuple-element.23.s0_ref), channel_id=1, source_target_pairs={{0,1},{1,2},{2,3},{3,0},{4,5},{5,6},{6,7},{7,4},{8,9},{9,10},{10,1... | collective-permute-start | bytes 36872 | tf_op jit(solution)/shard_map/ppermute | solution.py:498
  27.8 22.9 %all-to-all-start = ((f32[64,2,128]{2,1,0:T(2,128)}), f32[64,2,128]{2,1,0:T(2,128)S(1)}, u32[]{:S(2)}, u32[]{:S(2)}) async-start(f32[64,2,128]{2,1,0:T(2,128)} %get-tuple-element.30), calls=%async_computation | async-start | bytes 131072 | tf_op jit(solution)/shard_map/all_to_all | solution.py:558

commit v3 on v2

--- a/solution.py
+++ b/solution.py
@@ -18,7 +18,7 @@
 SLOT = 48
 HOME = 384
 STAYING = 4
-WINDOWS = (128, 160, 192, 256, 384, 512)
+WINDOWS = (128, 160, 192, 256, 320, 384, 448, 512)
 KEPT_ROWS = TILES * 192 + 576
 FAR_ROWS = 40000
 WIDTH_Q = 2560
@@ -33,6 +33,7 @@
 f32 = jnp.float32
 bf16 = jnp.bfloat16
 
+KEYS_AT = pl.ds(2 * KEPT_ROWS + SEQ, SEQ)
 VMEM = pl.BlockSpec(memory_space=pltpu.VMEM)
 SMEM = pl.BlockSpec(memory_space=pltpu.SMEM)
 HBM = pl.BlockSpec(memory_space=pltpu.HBM)
@@ -109,7 +110,17 @@
         out_ref[i : i + 1, :] = row_sums(fold(q * q))
 
 
-def layout_kernel(me_ref, len_ref, dest_ref, start_ref, tile_ref, doc_ref, stay_ref):
+AT_DEST, AT_SENT, AT_PLACE, AT_STAY = DOCS, 2 * DOCS, 3 * DOCS, 4 * DOCS
+
+
+def layout_kernel(
+    me_ref, len_ref, dest_ref, shift_ref, q_far, k_far, v_far,
+    start_ref, tile_ref, table_ref, q_near, k_near, v_near, sems,
+):
+    pairs = ((k_far, k_near), (v_far, v_near), (q_far, q_near))
+    copies = [pltpu.make_async_copy(a, b, sems.at[n]) for n, (a, b) in enumerate(pairs)]
+    for copy in copies:
+        copy.start()
     rows = start_ref.shape[0]
     position = lax.broadcasted_iota(jnp.int32, (rows, TILE), 0) * TILE + lax.broadcasted_iota(
         jnp.int32, (rows, TILE), 1
@@ -121,11 +132,14 @@
         end, start, kept, count, lows = carry
         length = len_ref[0, j]
         stays = dest_ref[0, j] == me
-        doc_ref[j] = end
-        slot = jnp.where(stays, jnp.minimum(count, STAYING - 1), STAYING)
-        stay_ref[slot] = end
-        stay_ref[8 + slot] = kept
-        stay_ref[16 + slot] = length
+        table_ref[j] = end
+        table_ref[AT_DEST + j] = dest_ref[0, j]
+        table_ref[AT_SENT + j] = jnp.where(stays, 0, length)
+        table_ref[AT_PLACE + j] = shift_ref[0, j]
+        slot = AT_STAY + jnp.where(stays, jnp.minimum(count, STAYING - 1), STAYING)
+        table_ref[slot] = end
+        table_ref[8 + slot] = kept
+        table_ref[16 + slot] = length
         kept = jnp.where(stays, kept + length, kept)
         count = jnp.where(stays, count + 1, count)
         end = end + length
@@ -138,6 +152,7 @@
         DOCS,
         step,
         (zero, jnp.zeros((rows, TILE), jnp.int32), zero, zero, (zero,) * TILES),
+        unroll=6,
     )
     start_ref[...] = start
     base = zero
@@ -150,6 +165,8 @@
         tile_ref[16 + i] = size
         tile_ref[32 + i] = base
         base = base + size
+    for copy in copies:
+        copy.wait()
 
 
 def window_of(tile_ref, i, size):
@@ -171,30 +188,68 @@
             body(size)
 
 
+def fill_slots(table_ref, lse_ref, slot_ref, home_ref, work):
+    lane = lax.broadcasted_iota(jnp.int32, (8, TILE), 1)
+    work[...] = jnp.zeros(work.shape, f32)
+    for j in range(DOCS):
+        dest = table_ref[AT_DEST + j]
+        length = table_ref[AT_SENT + j]
+        block = table_ref[j] >> 7
+        inner = table_ref[j] & (TILE - 1)
+        place = table_ref[AT_PLACE + j]
+        turn = (place - inner) & (TILE - 1)
+        here = pltpu.roll(lse_ref[block], turn, 1)
+        after = pltpu.roll(lse_ref[block + 1], turn, 1)
+        index = lane - place
+        value = jnp.where(index < TILE - inner, here, after)
+        work[dest] = jnp.where((index >= 0) & (index < length), value, 0.0)
+    heads = [work[:, h, :] for h in range(GROUP)]
+    wide = lax.broadcasted_iota(jnp.int32, (DEVICES, TILE), 1)
+    gap_low = (wide >= 48) & (wide < 64)
+    gap_high = wide >= 112
+    last = heads[4]
+    slot_ref[:, 0, :] = jnp.where(
+        gap_low,
+        pltpu.roll(last, 48, 1),
+        jnp.where(gap_high, pltpu.roll(last, 96, 1), heads[0] + pltpu.roll(heads[1], 64, 1)),
+    )
+    slot_ref[:, 1, :] = jnp.where(
+        gap_low, pltpu.roll(last, 16, 1), heads[2] + pltpu.roll(heads[3], 64, 1)
+    )
+    homes = [jnp.zeros((8, TILE), f32)] * (HOME // TILE)
+    for n in range(STAYING):
+        kept = table_ref[AT_STAY + 8 + n]
+        length = table_ref[AT_STAY + 16 + n]
+        gap = table_ref[AT_STAY + n] - kept
+        block = gap >> 7
+        inner = gap & (TILE - 1)
+        turn = (TILE - inner) & (TILE - 1)
+        moved = [pltpu.roll(lse_ref[block + b], turn, 1) for b in range(HOME // TILE + 1)]
+        for b in range(HOME // TILE):
+            value = jnp.where(lane < TILE - inner, moved[b], moved[b + 1])
+            column = lane + b * TILE
+            inside = (column >= kept) & (column < kept + length)
+            homes[b] = jnp.where(inside, value, homes[b])
+    home_ref[...] = jnp.concatenate(homes, axis=1)
+
+
 def stacked(ref, rows):
     return jnp.concatenate([ref[rows, h * HDIM : (h + 1) * HDIM] for h in range(GROUP)], axis=0)
 
 
 def scores_kernel(
-    tile_ref, start_ref, q_hbm, k_hbm, v_hbm, g_hbm, qg_ref, kg_ref, s0_ref, s1_ref, s2_ref, s3_ref,
-    kn_ref, recip_ref, lse_ref, kept_ref, dots_ref,
-    dot_acc, qn_ref, q_ref, g_ref, k_ref, v_ref, buf_ref, in_sems, thin_sems, qn_sems, sems,
+    tile_ref, table_ref, start_ref, q_ref, k_ref, v_ref, g_hbm, qg_ref, kg_ref, s0_ref, s1_ref, s2_ref, s3_ref,
+    recip_ref, kept_ref, dots_ref, slot_hbm, home_ref,
+    dot_acc, kn_ref, lse_ref, qn_ref, g_ref, buf_ref, work, slot_ref, in_sems, qn_sems, thin_sems, sems,
 ):
     per_chunk = TILES // CHUNKS
 
-    def arrival(which, c):
-        far, near = ((q_hbm, q_ref), (g_hbm, g_ref))[which]
+    def arrival(c):
         part = pl.ds(pl.multiple_of(c * CHUNK, CHUNK), CHUNK)
-        return pltpu.make_async_copy(far.at[part], near.at[part], in_sems.at[which, c])
-
-    k_copy = pltpu.make_async_copy(k_hbm, k_ref, thin_sems.at[0])
-    v_copy = pltpu.make_async_copy(v_hbm, v_ref, thin_sems.at[1])
-    k_copy.start()
+        return pltpu.make_async_copy(g_hbm.at[part], g_ref.at[part], in_sems.at[c])
+
     for c in range(CHUNKS):
-        arrival(0, c).start()
-    v_copy.start()
-    for c in range(CHUNKS):
-        arrival(1, c).start()
+        arrival(c).start()
     total = s0_ref[...] + s1_ref[...] + s2_ref[...] + s3_ref[...]
     recip = jnp.concatenate(
         [
@@ -207,27 +262,25 @@
     columns = turned(recip)
     lse_ref[TILES:] = jnp.zeros((lse_ref.shape[0] - TILES, 8, TILE), f32)
     dot_acc[...] = jnp.zeros(dot_acc.shape, f32)
-    k_copy.wait()
     for i in range(TILES):
         rows = slice(i * TILE, (i + 1) * TILE)
         col_k = columns[:, TILES + i : TILES + i + 1]
         kn_ref[rows, :] = (k_ref[rows, :].astype(f32) * col_k * kg_ref[...]).astype(bf16)
 
+    kn_copy = pltpu.make_async_copy(kn_ref, kept_ref.at[KEYS_AT, pl.ds(0, HDIM)], thin_sems.at[0])
+    kn_copy.start()
+
     def departure(c):
         near = pl.ds(pl.multiple_of(c * CHUNK, CHUNK), CHUNK)
         far = pl.ds(pl.multiple_of(2 * KEPT_ROWS + c * CHUNK, 32), CHUNK)
         return pltpu.make_async_copy(qn_ref.at[near], kept_ref.at[far], qn_sems.at[c])
 
     for i in range(TILES):
-        if i % per_chunk == 0:
-            arrival(0, i // per_chunk).wait()
         rows = slice(i * TILE, (i + 1) * TILE)
         col_q = columns[:, i : i + 1]
         qn_ref[rows, :] = (q_ref[rows, :].astype(f32) * col_q * qg_ref[...]).astype(bf16)
         if (i + 1) % per_chunk == 0:
             departure(i // per_chunk).start()
-    v_copy.wait()
-
     def copies(i, size):
         return [
             pltpu.make_async_copy(
@@ -244,7 +297,7 @@
 
         @pl.when(lax.rem(i, per_chunk) == 0)
         def _():
-            arrival(1, lax.div(i, per_chunk)).wait()
+            arrival(lax.div(i, per_chunk)).wait()
 
         def body(size):
             window = pl.ds(pl.multiple_of(tile_ref[i], 32), size)
@@ -280,8 +333,12 @@
         return carry
 
     lax.fori_loop(0, TILES, tile_step, 0)
+    fill_slots(table_ref, lse_ref, slot_ref, home_ref, work)
+    slot_copy = pltpu.make_async_copy(slot_ref, slot_hbm, thin_sems.at[1])
+    slot_copy.start()
     for i in range(TILES):
         dots_ref[TILES + i : TILES + i + 1, :] = row_sums(dot_acc[i * TILE : (i + 1) * TILE, :])
+    kn_copy.wait()
     for c in range(CHUNKS):
         departure(c).wait()
 
@@ -294,58 +351,11 @@
         return carry
 
     lax.fori_loop(0, TILES, drain, 0)
-
-
-def slot_kernel(
-    me_ref, doc_ref, stay_ref, len_ref, dest_ref, shift_ref, lse_ref, slot_ref, home_ref, work
-):
-    me = me_ref[0]
-    lane = lax.broadcasted_iota(jnp.int32, (8, TILE), 1)
-    work[...] = jnp.zeros(work.shape, f32)
-    for j in range(DOCS):
-        dest = dest_ref[0, j]
-        length = jnp.where(dest == me, 0, len_ref[0, j])
-        block = doc_ref[j] >> 7
-        inner = doc_ref[j] & (TILE - 1)
-        place = shift_ref[0, j]
-        turn = (place - inner) & (TILE - 1)
-        here = pltpu.roll(lse_ref[block], turn, 1)
-        after = pltpu.roll(lse_ref[block + 1], turn, 1)
-        index = lane - place
-        value = jnp.where(index < TILE - inner, here, after)
-        work[dest] = jnp.where((index >= 0) & (index < length), value, 0.0)
-    heads = [work[:, h, :] for h in range(GROUP)]
-    wide = lax.broadcasted_iota(jnp.int32, (DEVICES, TILE), 1)
-    gap_low = (wide >= 48) & (wide < 64)
-    gap_high = wide >= 112
-    last = heads[4]
-    slot_ref[:, 0, :] = jnp.where(
-        gap_low,
-        pltpu.roll(last, 48, 1),
-        jnp.where(gap_high, pltpu.roll(last, 96, 1), heads[0] + pltpu.roll(heads[1], 64, 1)),
-    )
-    slot_ref[:, 1, :] = jnp.where(
-        gap_low, pltpu.roll(last, 16, 1), heads[2] + pltpu.roll(heads[3], 64, 1)
-    )
-    homes = [jnp.zeros((8, TILE), f32)] * (HOME // TILE)
-    for n in range(STAYING):
-        kept = stay_ref[8 + n]
-        length = stay_ref[16 + n]
-        gap = stay_ref[n] - kept
-        block = gap >> 7
-        inner = gap & (TILE - 1)
-        turn = (TILE - inner) & (TILE - 1)
-        moved = [pltpu.roll(lse_ref[block + b], turn, 1) for b in range(HOME // TILE + 1)]
-        for b in range(HOME // TILE):
-            value = jnp.where(lane < TILE - inner, moved[b], moved[b + 1])
-            column = lane + b * TILE
-            inside = (column >= kept) & (column < kept + length)
-            homes[b] = jnp.where(inside, value, homes[b])
-    home_ref[...] = jnp.concatenate(homes, axis=1)
+    slot_copy.wait()
 
 
 def finish_kernel(
-    tile_ref, kn_hbm, kept_ref, g_hbm, q_hbm, k_hbm, qg_ref, kg_ref, recip_ref,
+    tile_ref, kept_ref, g_hbm, q_hbm, k_hbm, qg_ref, kg_ref, recip_ref,
     s0_ref, s1_ref, s2_ref, s3_ref,
     gq_ref, gk_ref, gv_ref,
     dk_acc, dv_acc, dq_buf, gq_buf, kn_ref, qn_ref, g_ref, q_ref, k_ref, gk_buf, gv_buf, buf_ref, cube_ref,
@@ -376,7 +386,7 @@
             for part in range(2)
         ]
 
-    kn_copy = pltpu.make_async_copy(kn_hbm, kn_ref, thin_sems.at[0])
+    kn_copy = pltpu.make_async_copy(kept_ref.at[KEYS_AT, pl.ds(0, HDIM)], kn_ref, thin_sems.at[0])
     k_copy = pltpu.make_async_copy(k_hbm, k_ref, thin_sems.at[1])
     gk_copy = pltpu.make_async_copy(gk_buf, gk_ref, thin_sems.at[2])
     gv_copy = pltpu.make_async_copy(gv_buf, gv_ref, thin_sems.at[3])
@@ -507,7 +517,6 @@
     stat = ((2 * TILES, TILE), f32)
     wide = ((SEQ, GROUP * HDIM), bf16)
     thin = ((SEQ, HDIM), bf16)
-    logs = ((16, 8, TILE), f32)
     kept = ((FAR_ROWS, GROUP * HDIM), bf16)
 
     (squares,) = call(
@@ -518,48 +527,51 @@
         vmem=53.7,
         name="squares",
     )(q_raw, k_raw)
-    start, tiles, docs, stays = call(
+    start, tiles, table, q_near, k_near, v_near = call(
         layout_kernel,
-        [((16, TILE), jnp.int32), ((48,), jnp.int32), ((DOCS,), jnp.int32), ((24,), jnp.int32)],
-        [SMEM] * 3,
-        [VMEM] + [SMEM] * 3,
+        [
+            ((16, TILE), jnp.int32),
+            ((48,), jnp.int32),
+            ((AT_STAY + 24,), jnp.int32),
+            wide,
+            thin,
+            thin,
+        ],
+        [SMEM] * 4 + [HBM] * 3,
+        [VMEM] + [SMEM] * 2 + [HBM] * 3,
+        scratch=[pltpu.SemaphoreType.DMA((3,))],
+        vmem=50.5,
         name="layout",
-    )(me, doc_lengths, plan_dest)
-    kn, recip, lse, kept, dots = call(
+    )(me, doc_lengths, plan_dest, plan_offset, q_raw, k_raw, v_proj)
+    recip, kept, dots, slots, home = call(
         scores_kernel,
-        [thin, stat, logs, kept, stat],
-        [SMEM, VMEM] + [HBM] * 4 + [VMEM] * 6,
-        out_specs=[VMEM] * 3 + [HBM, VMEM],
+        [stat, kept, stat, ((DEVICES, 2, TILE), f32), ((8, HOME), f32)],
+        [SMEM] * 2 + [VMEM] * 4 + [HBM] + [VMEM] * 6,
+        out_specs=[VMEM, HBM, VMEM, HBM, VMEM],
         scratch=[
             pltpu.VMEM((SEQ, HDIM), f32),
+            pltpu.VMEM(*thin),
+            pltpu.VMEM((16, 8, TILE), f32),
             pltpu.VMEM(*wide),
             pltpu.VMEM(*wide),
-            pltpu.VMEM(*wide),
-            pltpu.VMEM(*thin),
-            pltpu.VMEM(*thin),
             pltpu.VMEM((2 * KEPT_ROWS, GROUP * HDIM), bf16),
-            pltpu.SemaphoreType.DMA((2, CHUNKS)),
+            pltpu.VMEM((DEVICES, 8, TILE), f32),
+            pltpu.VMEM((DEVICES, 2, TILE), f32),
+            pltpu.SemaphoreType.DMA((CHUNKS,)),
+            pltpu.SemaphoreType.DMA((CHUNKS,)),
             pltpu.SemaphoreType.DMA((2,)),
-            pltpu.SemaphoreType.DMA((CHUNKS,)),
             pltpu.SemaphoreType.DMA((2, TILES)),
         ],
         flops=10**9,
-        vmem=53.7,
+        vmem=50.5,
         name="scores",
-    )(tiles, start, q_raw, k_raw, v_proj, d_out, qg, kg, *from_others(squares))
+    )(tiles, table, start, q_near, k_near, v_near, d_out, qg, kg, *from_others(squares))
     all_dots = from_others(dots)
-    slots, home = call(
-        slot_kernel,
-        [((DEVICES, 2, TILE), f32), ((8, HOME), f32)],
-        [SMEM] * 6 + [VMEM],
-        scratch=[pltpu.VMEM((DEVICES, 8, TILE), f32)],
-        name="slots",
-    )(me, docs, stays, doc_lengths, plan_dest, plan_offset, lse)
     got = lax.all_to_all(slots, "dp", split_axis=0, concat_axis=0, tiled=True)
     grad_q, grad_k, grad_v = call(
         finish_kernel,
         [wide, thin, thin],
-        [SMEM] + [HBM] * 5 + [VMEM] * 7,
+        [SMEM] + [HBM] * 4 + [VMEM] * 7,
         out_specs=[HBM] * 3,
         scratch=[
             pltpu.VMEM((SEQ, HDIM), f32),
@@ -583,7 +595,7 @@
         flops=10**10,
         vmem=53.7,
         name="finish",
-    )(tiles, kn, kept, d_out, q_raw, k_raw, qg, kg, recip, *all_dots)
+    )(tiles, kept, d_out, q_raw, k_raw, qg, kg, recip, *all_dots)
     (balanced,) = call(
         assemble_kernel,
         [((GROUP, HOME + DEVICES * SLOT), f32)],

time: 52.3 us -> 49.6 us (0.948)
  Pallas kernels: 29 us -> 24.9 us
  starting transfers between devices: 20.2 us -> 22 us
    pallas_call x4 -> x3, Pallas kernels: 26 us -> 21.9 us  [the longest x1 10.2 us: local(): call(scores_kernel, [stat, kept, stat, ((DEVICES, 2, TILE), f32), ((8, HO...]
    all_to_all x1, starting transfers between devices: 12.8 us -> 13.8 us  [local(): got = lax.all_to_all(slots, 'dp', split_axis=0, concat_axis=0, tiled=True)]
    ppermute x6, waiting for transfers between devices: 0.89 us -> 0.02 us  [from_others(): lax.ppermute(values, 'head', [(i, (i + s) % size) for i in range(size)])]
    ppermute x6, starting transfers between devices: 7.32 us -> 8.16 us  [from_others(): lax.ppermute(values, 'head', [(i, (i + s) % size) for i in range(size)])]
    all_to_all x1, waiting for transfers between devices: 0.93 us -> 1.48 us  [local(): got = lax.all_to_all(slots, 'dp', split_axis=0, concat_axis=0, tiled=True)]
  transfers between devices with their start and end apart: 7 -> 7, of which waited for: 3 -> 1; matrix products, arithmetic and copies ran while one was open for 0% -> 0% of each run, Pallas kernels for 25% -> 24%
where the time goes in v3:
time: 49.6 us; the launch traced here: 49.2 us
  Pallas kernels  24.9 us (50%)
  starting transfers between devices  22 us (44%)
  waiting for transfers between devices  1.49 us (3%)
  between operations  0.82 us (2%)
    all_to_all x1, starting transfers between devices, local(): got = lax.all_to_all(slots, 'dp', split_axis=0, concat_axis=0, tiled=True)  13.8 us
    pallas_call x1, Pallas kernels, local(): call(scores_kernel, [stat, kept, stat, ((DEVICES, 2, TILE), f32), ((8, HO...  10.2 us
    pallas_call x1, Pallas kernels, local(): call(finish_kernel, [wide, thin, thin], [SMEM] + [HBM] * 4 + [VMEM] * 7,...  8.57 us
    ppermute x6, starting transfers between devices, from_others(): lax.ppermute(values, 'head', [(i, (i + s) % size) for i in range(size)])  8.16 us
    pallas_call x1, Pallas kernels, local(): call(layout_kernel, [((16, TILE), jnp.int32), ((48,), jnp.int32), ((AT_ST...  3.11 us
    pallas_call x1, Pallas kernels, local(): call(square_kernel, [stat], [HBM] * 2, scratch=[pltpu.VMEM(*wide), pltpu....  2.07 us
    all_to_all x1, waiting for transfers between devices, local(): got = lax.all_to_all(slots, 'dp', split_axis=0, concat_axis=0, tiled=True)  1.48 us
  transfers between devices with their start and end apart: 7, of which 1 were waited for; matrix products, arithmetic and copies ran while one was open for 0% of the time, Pallas kernels for 24%

profile of v3, /device:TPU:1, one launch (start us, length us, event | category | flops | bytes accessed | tf_op | source)
XLA Modules:
  0.0 49.2 jit_solution(14718733057838029934)
XLA Ops:
  0.6 0.0 copy-start
  0.6 0.0 copy-start.6
  0.7 0.0 copy-start.5
  0.7 0.0 copy-start.4
  0.7 2.1 %squares.1.s0_ref = f32[24,128]{1,0:T(8,128)S(1)} custom-call(bf16[1536,640]{1,0:T(8,128)(2,1)} %q_hbm.1, bf16[1536,128]{1,0:T(8,128)(2,1)} %k_hbm.1), custom_call_target="tpu_custom_call" | custom-call | flops 10000000 | bytes 1000000 | tf_op jit(solution)/shard_map/squares/pallas_call | solution.py:522
  2.8 0.0 copy-start.2
  2.8 3.6 %collective-permute-start.2 = (f32[24,128]{1,0:T(8,128)S(1)}, f32[24,128]{1,0:T(8,128)S(1)}, u32[]{:S(2)}, u32[]{:S(2)}) collective-permute-start(f32[24,128]{1,0:T(8,128)S(1)} %squares.1.s0_ref), channel_id=1, source_target_pairs={{0,3},{1,0},{2,1},{3,2},{4,7},{5,4},{6,5},{7,6},{8,11},{9,8},{10,9... | collective-permute-start | bytes 36872 | tf_op jit(solution)/shard_map/ppermute | solution.py:508
  6.4 0.3 collective-permute-start.1
  6.8 0.7 %collective-permute-start = (f32[24,128]{1,0:T(8,128)S(1)}, f32[24,128]{1,0:T(8,128)S(1)}, u32[]{:S(2)}, u32[]{:S(2)}) collective-permute-start(f32[24,128]{1,0:T(8,128)S(1)} %squares.1.s0_ref), channel_id=1, source_target_pairs={{0,1},{1,2},{2,3},{3,0},{4,5},{5,6},{6,7},{7,4},{8,9},{9,10},{10,1... | collective-permute-start | bytes 36872 | tf_op jit(solution)/shard_map/ppermute | solution.py:508
  7.5 3.1 %layout.1 = (s32[16,128]{1,0:T(8,128)S(1)}, s32[48]{0:T(128)S(1)}, s32[168]{0:T(256)S(1)}, bf16[1536,640]{1,0:T(8,128)(2,1)S(1)}, bf16[1536,128]{1,0:T(8,128)(2,1)S(1)}, /*index=5*/bf16[1536,128]{1,0:T(8,128)(2,1)S(1)}) custom-call(s32[1]{0:T(128)} %bitcast.me_ref, s32[1,36]{1,0:T(1,128)S(1)} %copy-done.3, s32[1,36]{1,0:T(1,128)S(1)} %copy-done.4, ...), custom_call_target="tpu_custom_call" | custom-call | flops 10000000 | bytes 1000000 | tf_op jit(solution)/shard_map/layout/pallas_call | solution.py:530
  10.6 0.0 collective-permute-done.2.s3_ref
  10.6 0.0 collective-permute-done.1.s2_ref
  10.7 0.0 collective-permute-done.s1_ref
  10.7 10.2 %scores.1 = (f32[24,128]{1,0:T(8,128)S(1)}, bf16[40000,640]{1,0:T(8,128)(2,1)}, f32[24,128]{1,0:T(8,128)S(1)}, f32[64,2,128]{2,1,0:T(2,128)}, f32[8,384]{1,0:T(8,128)S(1)}) custom-call(s32[48]{0:T(128)S(1)} %get-tuple-element.18.tile_ref, s32[168]{0:T(256)S(1)} %get-tuple-element.19.table_ref, s32[16,128]{1,0:T(8,128)S(1)} %get-tuple-element.20.start_ref, ...), custom_call_target="tpu_custom_call" | custom-call | flops 1000000000 | bytes 1000000 | tf_op jit(solution)/shard_map/scores/pallas_call | solution.py:546
  20.9 2.1 %collective-permute-start.5 = (f32[24,128]{1,0:T(8,128)S(1)}, f32[24,128]{1,0:T(8,128)S(1)}, u32[]{:S(2)}, u32[]{:S(2)}) collective-permute-start(f32[24,128]{1,0:T(8,128)S(1)} %get-tuple-element.26.s0_ref), channel_id=1, source_target_pairs={{0,3},{1,0},{2,1},{3,2},{4,7},{5,4},{6,5},{7,6},{8,11},{9,8},{10,9... | collective-permute-start | bytes 36872 | tf_op jit(solution)/shard_map/ppermute | solution.py:508
  22.9 1.4 %collective-permute-start.4 = (f32[24,128]{1,0:T(8,128)S(1)}, f32[24,128]{1,0:T(8,128)S(1)}, u32[]{:S(2)}, u32[]{:S(2)}) collective-permute-start(f32[24,128]{1,0:T(8,128)S(1)} %get-tuple-element.26.s0_ref), channel_id=1, source_target_pairs={{0,2},{1,3},{2,0},{3,1},{4,6},{5,7},{6,4},{7,5},{8,10},{9,11},{10,... | collective-permute-start | bytes 36872 | tf_op jit(solution)/shard_map/ppermute | solution.py:508
  24.3 0.0 collective-permute-start.3
  24.3 13.8 %all-to-all-start = ((f32[64,2,128]{2,1,0:T(2,128)}), f32[64,2,128]{2,1,0:T(2,128)S(1)}, u32[]{:S(2)}, u32[]{:S(2)}) async-start(f32[64,2,128]{2,1,0:T(2,128)} %get-tuple-element.30), calls=%async_computation | async-start | bytes 131072 | tf_op jit(solution)/shard_map/all_to_all | solution.py:570
  38.2 0.0 collective-permute-done.5.s3_ref
  38.2 0.0 collective-permute-done.4.s2_ref
  38.2 0.0 collective-permute-done.3.s1_ref
  38.2 8.6 %finish.1 = (bf16[1536,640]{1,0:T(8,128)(2,1)}, bf16[1536,128]{1,0:T(8,128)(2,1)}, bf16[1536,128]{1,0:T(8,128)(2,1)}) custom-call(s32[48]{0:T(128)S(1)} %get-tuple-element.18.tile_ref, bf16[40000,640]{1,0:T(8,128)(2,1)} %get-tuple-element.24.kept_ref, bf16[1536,640]{1,0:T(8,128)(2,1)} %g_hbm.3, bf16[1536,640]{1,0:T(8,128)(2,1)} %q_hbm.1, ...), custom_call_target="tpu_custom_call" | custom-call | flops 10000000000 | bytes 1000000 | tf_op jit(solution)/shard_map/finish/pallas_call | solution.py:571
  46.8 1.5 %all-to-all-done.got_ref = f32[64,2,128]{2,1,0:T(2,128)S(1)} async-done(((f32[64,2,128]{2,1,0:T(2,128)}), f32[64,2,128]{2,1,0:T(2,128)S(1)}, u32[]{:S(2)}, u32[]{:S(2)}) %all-to-all-start) | async-done | bytes 65568 | tf_op jit(solution)/shard_map/all_to_all | solution.py:570
  48.3 0.9 %assemble.1 = f32[5,3456]{1,0:T(8,128)} custom-call(f32[64,2,128]{2,1,0:T(2,128)S(1)} %all-to-all-done.got_ref, f32[8,384]{1,0:T(8,128)S(1)} %get-tuple-element.31.home_ref), custom_call_target="tpu_custom_call" | custom-call | flops 10000000 | bytes 1000000 | tf_op jit(solution)/shard_map/assemble/pallas_call | solution.py:599
  (10 shorter events, 0.0 us)
Async XLA Ops:
  0.6 6.8 %copy-start = (bf16[1536,128]{1,0:T(8,128)(2,1)S(1)}, bf16[1536,128]{1,0:T(8,128)(2,1)}, u32[]{:S(2)}) copy-start(bf16[1536,128]{1,0:T(8,128)(2,1)} %k_hbm.1) | copy-start | bytes 1179652
  0.6 6.8 %copy-start.6 = (f32[640]{0:T(1024)S(1)}, f32[640]{0:T(1024)}, u32[]{:S(2)}) copy-start(f32[640]{0:T(1024)} %param.13) | copy-start | bytes 7684
  0.7 6.8 %copy-start.5 = (s32[1,36]{1,0:T(1,128)S(1)}, s32[1,36]{1,0:T(1,128)}, u32[]{:S(2)}) copy-start(s32[1,36]{1,0:T(1,128)} %shift_ref.1) | copy-start | bytes 436
  0.7 6.8 %copy-start.4 = (s32[1,36]{1,0:T(1,128)S(1)}, s32[1,36]{1,0:T(1,128)}, u32[]{:S(2)}) copy-start(s32[1,36]{1,0:T(1,128)} %dest_ref.1) | copy-start | bytes 436
  0.7 6.8 %copy-start.3 = (s32[1,36]{1,0:T(1,128)S(1)}, s32[1,36]{1,0:T(1,128)}, u32[]{:S(2)}) copy-start(s32[1,36]{1,0:T(1,128)} %len_ref.1) | copy-start | bytes 436
  0.7 6.8 %copy-start.1 = (bf16[1536,128]{1,0:T(8,128)(2,1)S(1)}, bf16[1536,128]{1,0:T(8,128)(2,1)}, u32[]{:S(2)}) copy-start(bf16[1536,128]{1,0:T(8,128)(2,1)} %v_far.1) | copy-start | bytes 1179652
  2.8 7.9 %copy-start.2 = (f32[128]{0:T(128)S(1)}, f32[128]{0:T(128)}, u32[]{:S(2)}) copy-start(f32[128]{0:T(128)} %param.14) | copy-start | bytes 1540
  2.8 7.9 %collective-permute-start.2 = (f32[24,128]{1,0:T(8,128)S(1)}, f32[24,128]{1,0:T(8,128)S(1)}, u32[]{:S(2)}, u32[]{:S(2)}) collective-permute-start(f32[24,128]{1,0:T(8,128)S(1)} %squares.1.s0_ref), channel_id=1, source_target_pairs={{0,3},{1,0},{2,1},{3,2},{4,7},{5,4},{6,5},{7,6},{8,11},{9,8},{10,9... | collective-permute-start | bytes 36872 | tf_op jit(solution)/shard_map/ppermute | solution.py:508
  6.4 4.2 %collective-permute-start.1 = (f32[24,128]{1,0:T(8,128)S(1)}, f32[24,128]{1,0:T(8,128)S(1)}, u32[]{:S(2)}, u32[]{:S(2)}) collective-permute-start(f32[24,128]{1,0:T(8,128)S(1)} %squares.1.s0_ref), channel_id=1, source_target_pairs={{0,2},{1,3},{2,0},{3,1},{4,6},{5,7},{6,4},{7,5},{8,10},{9,11},{10,... | collective-permute-start | bytes 36872 | tf_op jit(solution)/shard_map/ppermute | solution.py:508
  6.8 3.9 %collective-permute-start = (f32[24,128]{1,0:T(8,128)S(1)}, f32[24,128]{1,0:T(8,128)S(1)}, u32[]{:S(2)}, u32[]{:S(2)}) collective-permute-start(f32[24,128]{1,0:T(8,128)S(1)} %squares.1.s0_ref), channel_id=1, source_target_pairs={{0,1},{1,2},{2,3},{3,0},{4,5},{5,6},{6,7},{7,4},{8,9},{9,10},{10,1... | collective-permute-start | bytes 36872 | tf_op jit(solution)/shard_map/ppermute | solution.py:508
  20.9 17.3 %collective-permute-start.5 = (f32[24,128]{1,0:T(8,128)S(1)}, f32[24,128]{1,0:T(8,128)S(1)}, u32[]{:S(2)}, u32[]{:S(2)}) collective-permute-start(f32[24,128]{1,0:T(8,128)S(1)} %get-tuple-element.26.s0_ref), channel_id=1, source_target_pairs={{0,3},{1,0},{2,1},{3,2},{4,7},{5,4},{6,5},{7,6},{8,11},{9,8},{10,9... | collective-permute-start | bytes 36872 | tf_op jit(solution)/shard_map/ppermute | solution.py:508
  22.9 15.3 %collective-permute-start.4 = (f32[24,128]{1,0:T(8,128)S(1)}, f32[24,128]{1,0:T(8,128)S(1)}, u32[]{:S(2)}, u32[]{:S(2)}) collective-permute-start(f32[24,128]{1,0:T(8,128)S(1)} %get-tuple-element.26.s0_ref), channel_id=1, source_target_pairs={{0,2},{1,3},{2,0},{3,1},{4,6},{5,7},{6,4},{7,5},{8,10},{9,11},{10,... | collective-permute-start | bytes 36872 | tf_op jit(solution)/shard_map/ppermute | solution.py:508
  24.3 13.9 %collective-permute-start.3 = (f32[24,128]{1,0:T(8,128)S(1)}, f32[24,128]{1,0:T(8,128)S(1)}, u32[]{:S(2)}, u32[]{:S(2)}) collective-permute-start(f32[24,128]{1,0:T(8,128)S(1)} %get-tuple-element.26.s0_ref), channel_id=1, source_target_pairs={{0,1},{1,2},{2,3},{3,0},{4,5},{5,6},{6,7},{7,4},{8,9},{9,10},{10,1... | collective-permute-start | bytes 36872 | tf_op jit(solution)/shard_map/ppermute | solution.py:508
  24.3 23.9 %all-to-all-start = ((f32[64,2,128]{2,1,0:T(2,128)}), f32[64,2,128]{2,1,0:T(2,128)S(1)}, u32[]{:S(2)}, u32[]{:S(2)}) async-start(f32[64,2,128]{2,1,0:T(2,128)} %get-tuple-element.30), calls=%async_computation | async-start | bytes 131072 | tf_op jit(solution)/shard_map/all_to_all | solution.py:570

commit v4 on v3

--- a/solution.py
+++ b/solution.py
@@ -114,13 +114,11 @@
 
 
 def layout_kernel(
-    me_ref, len_ref, dest_ref, shift_ref, q_far, k_far, v_far,
-    start_ref, tile_ref, table_ref, q_near, k_near, v_near, sems,
+    me_ref, len_ref, dest_ref, shift_ref, q_far,
+    start_ref, tile_ref, table_ref, q_near, sem,
 ):
-    pairs = ((k_far, k_near), (v_far, v_near), (q_far, q_near))
-    copies = [pltpu.make_async_copy(a, b, sems.at[n]) for n, (a, b) in enumerate(pairs)]
-    for copy in copies:
-        copy.start()
+    copy = pltpu.make_async_copy(q_far, q_near, sem)
+    copy.start()
     rows = start_ref.shape[0]
     position = lax.broadcasted_iota(jnp.int32, (rows, TILE), 0) * TILE + lax.broadcasted_iota(
         jnp.int32, (rows, TILE), 1
@@ -165,8 +163,7 @@
         tile_ref[16 + i] = size
         tile_ref[32 + i] = base
         base = base + size
-    for copy in copies:
-        copy.wait()
+    copy.wait()
 
 
 def window_of(tile_ref, i, size):
@@ -527,22 +524,20 @@
         vmem=53.7,
         name="squares",
     )(q_raw, k_raw)
-    start, tiles, table, q_near, k_near, v_near = call(
+    start, tiles, table, q_near = call(
         layout_kernel,
         [
             ((16, TILE), jnp.int32),
             ((48,), jnp.int32),
             ((AT_STAY + 24,), jnp.int32),
             wide,
-            thin,
-            thin,
         ],
-        [SMEM] * 4 + [HBM] * 3,
-        [VMEM] + [SMEM] * 2 + [HBM] * 3,
-        scratch=[pltpu.SemaphoreType.DMA((3,))],
+        [SMEM] * 4 + [HBM],
+        [VMEM] + [SMEM] * 2 + [HBM],
+        scratch=[pltpu.SemaphoreType.DMA],
         vmem=50.5,
         name="layout",
-    )(me, doc_lengths, plan_dest, plan_offset, q_raw, k_raw, v_proj)
+    )(me, doc_lengths, plan_dest, plan_offset, q_raw)
     recip, kept, dots, slots, home = call(
         scores_kernel,
         [stat, kept, stat, ((DEVICES, 2, TILE), f32), ((8, HOME), f32)],
@@ -565,7 +560,7 @@
         flops=10**9,
         vmem=50.5,
         name="scores",
-    )(tiles, table, start, q_near, k_near, v_near, d_out, qg, kg, *from_others(squares))
+    )(tiles, table, start, q_near, k_raw, v_proj, d_out, qg, kg, *from_others(squares))
     all_dots = from_others(dots)
     got = lax.all_to_all(slots, "dp", split_axis=0, concat_axis=0, tiled=True)
     grad_q, grad_k, grad_v = call(

time: 49.6 us -> 49.9 us (level); the launches traced: 49.2 us -> 50.1 us
  starting transfers between devices: 22 us -> 22.5 us
    all_to_all x1, starting transfers between devices: 13.8 us -> 14.7 us  [local(): got = lax.all_to_all(slots, 'dp', split_axis=0, concat_axis=0, tiled=True)]
  transfers between devices with their start and end apart: 7 -> 7, of which waited for: 1 -> 3; matrix products, arithmetic and copies ran while one was open for 0% -> 0% of each run, Pallas kernels for 24% -> 23%
where the time goes in v4:
time: 49.9 us; the launch traced here: 50.1 us
  Pallas kernels  25.1 us (50%)
  starting transfers between devices  22.5 us (45%)
  waiting for transfers between devices  1.66 us (3%)
  between operations  0.79 us (2%)
    all_to_all x1, starting transfers between devices, local(): got = lax.all_to_all(slots, 'dp', split_axis=0, concat_axis=0, tiled=True)  14.7 us
    pallas_call x1, Pallas kernels, local(): call(scores_kernel, [stat, kept, stat, ((DEVICES, 2, TILE), f32), ((8, HO...  10.6 us
    pallas_call x1, Pallas kernels, local(): call(finish_kernel, [wide, thin, thin], [SMEM] + [HBM] * 4 + [VMEM] * 7,...  8.77 us
    ppermute x6, starting transfers between devices, from_others(): lax.ppermute(values, 'head', [(i, (i + s) % size) for i in range(size)])  7.84 us
    pallas_call x1, Pallas kernels, local(): call(layout_kernel, [((16, TILE), jnp.int32), ((48,), jnp.int32), ((AT_ST...  2.72 us
    pallas_call x1, Pallas kernels, local(): call(square_kernel, [stat], [HBM] * 2, scratch=[pltpu.VMEM(*wide), pltpu....  2.1 us
    all_to_all x1, waiting for transfers between devices, local(): got = lax.all_to_all(slots, 'dp', split_axis=0, concat_axis=0, tiled=True)  1.28 us
  transfers between devices with their start and end apart: 7, of which 3 were waited for; matrix products, arithmetic and copies ran while one was open for 0% of the time, Pallas kernels for 23%

profile of v4, /device:TPU:1, one launch (start us, length us, event | category | flops | bytes accessed | tf_op | source)
XLA Modules:
  0.0 50.1 jit_solution(3778589061981719624)
XLA Ops:
  0.6 0.0 copy-start
  0.6 0.0 copy-start.6
  0.7 0.0 copy-start.5
  0.7 2.1 %squares.1.s0_ref = f32[24,128]{1,0:T(8,128)S(1)} custom-call(bf16[1536,640]{1,0:T(8,128)(2,1)} %q_hbm.1, bf16[1536,128]{1,0:T(8,128)(2,1)} %k_hbm.1), custom_call_target="tpu_custom_call" | custom-call | flops 10000000 | bytes 1000000 | tf_op jit(solution)/shard_map/squares/pallas_call | solution.py:519
  2.8 3.6 %collective-permute-start.2 = (f32[24,128]{1,0:T(8,128)S(1)}, f32[24,128]{1,0:T(8,128)S(1)}, u32[]{:S(2)}, u32[]{:S(2)}) collective-permute-start(f32[24,128]{1,0:T(8,128)S(1)} %squares.1.s0_ref), channel_id=1, source_target_pairs={{0,3},{1,0},{2,1},{3,2},{4,7},{5,4},{6,5},{7,6},{8,11},{9,8},{10,9... | collective-permute-start | bytes 36872 | tf_op jit(solution)/shard_map/ppermute | solution.py:505
  6.5 0.3 collective-permute-start.1
  6.8 0.7 %collective-permute-start = (f32[24,128]{1,0:T(8,128)S(1)}, f32[24,128]{1,0:T(8,128)S(1)}, u32[]{:S(2)}, u32[]{:S(2)}) collective-permute-start(f32[24,128]{1,0:T(8,128)S(1)} %squares.1.s0_ref), channel_id=1, source_target_pairs={{0,1},{1,2},{2,3},{3,0},{4,5},{5,6},{6,7},{7,4},{8,9},{9,10},{10,1... | collective-permute-start | bytes 36872 | tf_op jit(solution)/shard_map/ppermute | solution.py:505
  7.5 0.0 copy-done.4
  7.5 0.0 copy-done.3
  7.5 2.7 %layout.1 = (s32[16,128]{1,0:T(8,128)S(1)}, s32[48]{0:T(128)S(1)}, s32[168]{0:T(256)S(1)}, bf16[1536,640]{1,0:T(8,128)(2,1)S(1)}) custom-call(s32[1]{0:T(128)} %bitcast.me_ref, s32[1,36]{1,0:T(1,128)S(1)} %copy-done.3, s32[1,36]{1,0:T(1,128)S(1)} %copy-done.4, s32[1,36]{1,0:T(1,128)S(1)} %copy-done.5, bf16[1536,640]{1,0:T(8,128)(2,1)} %q_hbm.1), custom_call_target="tpu_custom_call" | custom-call | flops 10000000 | bytes 1000000 | tf_op jit(solution)/shard_map/layout/pallas_call | solution.py:527
  10.3 0.0 collective-permute-done.2.s3_ref
  10.3 0.2 collective-permute-done.1.s2_ref
  10.5 0.1 collective-permute-done.s1_ref
  10.6 10.6 %scores.1 = (f32[24,128]{1,0:T(8,128)S(1)}, bf16[40000,640]{1,0:T(8,128)(2,1)}, f32[24,128]{1,0:T(8,128)S(1)}, f32[64,2,128]{2,1,0:T(2,128)}, f32[8,384]{1,0:T(8,128)S(1)}) custom-call(s32[48]{0:T(128)S(1)} %get-tuple-element.16.tile_ref, s32[168]{0:T(256)S(1)} %get-tuple-element.17.table_ref, s32[16,128]{1,0:T(8,128)S(1)} %get-tuple-element.18.start_ref, ...), custom_call_target="tpu_custom_call" | custom-call | flops 1000000000 | bytes 1000000 | tf_op jit(solution)/shard_map/scores/pallas_call | solution.py:541
  21.3 1.7 %collective-permute-start.5 = (f32[24,128]{1,0:T(8,128)S(1)}, f32[24,128]{1,0:T(8,128)S(1)}, u32[]{:S(2)}, u32[]{:S(2)}) collective-permute-start(f32[24,128]{1,0:T(8,128)S(1)} %get-tuple-element.22.s0_ref), channel_id=1, source_target_pairs={{0,3},{1,0},{2,1},{3,2},{4,7},{5,4},{6,5},{7,6},{8,11},{9,8},{10,9... | collective-permute-start | bytes 36872 | tf_op jit(solution)/shard_map/ppermute | solution.py:505
  23.0 1.4 %collective-permute-start.4 = (f32[24,128]{1,0:T(8,128)S(1)}, f32[24,128]{1,0:T(8,128)S(1)}, u32[]{:S(2)}, u32[]{:S(2)}) collective-permute-start(f32[24,128]{1,0:T(8,128)S(1)} %get-tuple-element.22.s0_ref), channel_id=1, source_target_pairs={{0,2},{1,3},{2,0},{3,1},{4,6},{5,7},{6,4},{7,5},{8,10},{9,11},{10,... | collective-permute-start | bytes 36872 | tf_op jit(solution)/shard_map/ppermute | solution.py:505
  24.4 0.0 collective-permute-start.3
  24.4 14.7 %all-to-all-start = ((f32[64,2,128]{2,1,0:T(2,128)}), f32[64,2,128]{2,1,0:T(2,128)S(1)}, u32[]{:S(2)}, u32[]{:S(2)}) async-start(f32[64,2,128]{2,1,0:T(2,128)} %get-tuple-element.26), calls=%async_computation | async-start | bytes 131072 | tf_op jit(solution)/shard_map/all_to_all | solution.py:565
  39.1 0.0 collective-permute-done.5.s3_ref
  39.1 0.0 collective-permute-done.4.s2_ref
  39.1 0.0 collective-permute-done.3.s1_ref
  39.1 8.8 %finish.1 = (bf16[1536,640]{1,0:T(8,128)(2,1)}, bf16[1536,128]{1,0:T(8,128)(2,1)}, bf16[1536,128]{1,0:T(8,128)(2,1)}) custom-call(s32[48]{0:T(128)S(1)} %get-tuple-element.16.tile_ref, bf16[40000,640]{1,0:T(8,128)(2,1)} %get-tuple-element.20.kept_ref, bf16[1536,640]{1,0:T(8,128)(2,1)} %g_hbm.3, bf16[1536,640]{1,0:T(8,128)(2,1)} %q_hbm.1, ...), custom_call_target="tpu_custom_call" | custom-call | flops 10000000000 | bytes 1000000 | tf_op jit(solution)/shard_map/finish/pallas_call | solution.py:566
  47.9 1.3 %all-to-all-done.got_ref = f32[64,2,128]{2,1,0:T(2,128)S(1)} async-done(((f32[64,2,128]{2,1,0:T(2,128)}), f32[64,2,128]{2,1,0:T(2,128)S(1)}, u32[]{:S(2)}, u32[]{:S(2)}) %all-to-all-start) | async-done | bytes 65568 | tf_op jit(solution)/shard_map/all_to_all | solution.py:565
  49.2 0.9 %assemble.1 = f32[5,3456]{1,0:T(8,128)} custom-call(f32[64,2,128]{2,1,0:T(2,128)S(1)} %all-to-all-done.got_ref, f32[8,384]{1,0:T(8,128)S(1)} %get-tuple-element.27.home_ref), custom_call_target="tpu_custom_call" | custom-call | flops 10000000 | bytes 1000000 | tf_op jit(solution)/shard_map/assemble/pallas_call | solution.py:594
  (10 shorter events, 0.0 us)
Async XLA Ops:
  0.6 10.0 %copy-start = (bf16[1536,128]{1,0:T(8,128)(2,1)S(1)}, bf16[1536,128]{1,0:T(8,128)(2,1)}, u32[]{:S(2)}) copy-start(bf16[1536,128]{1,0:T(8,128)(2,1)} %k_hbm.1) | copy-start | bytes 1179652
  0.6 6.9 %copy-start.6 = (f32[640]{0:T(1024)S(1)}, f32[640]{0:T(1024)}, u32[]{:S(2)}) copy-start(f32[640]{0:T(1024)} %param.13) | copy-start | bytes 7684
  0.7 6.9 %copy-start.5 = (s32[1,36]{1,0:T(1,128)S(1)}, s32[1,36]{1,0:T(1,128)}, u32[]{:S(2)}) copy-start(s32[1,36]{1,0:T(1,128)} %shift_ref.1) | copy-start | bytes 436
  0.7 6.8 %copy-start.4 = (s32[1,36]{1,0:T(1,128)S(1)}, s32[1,36]{1,0:T(1,128)}, u32[]{:S(2)}) copy-start(s32[1,36]{1,0:T(1,128)} %dest_ref.1) | copy-start | bytes 436
  0.7 6.8 %copy-start.3 = (s32[1,36]{1,0:T(1,128)S(1)}, s32[1,36]{1,0:T(1,128)}, u32[]{:S(2)}) copy-start(s32[1,36]{1,0:T(1,128)} %len_ref.1) | copy-start | bytes 436
  0.7 10.0 %copy-start.2 = (f32[128]{0:T(128)S(1)}, f32[128]{0:T(128)}, u32[]{:S(2)}) copy-start(f32[128]{0:T(128)} %param.14) | copy-start | bytes 1540
  0.7 10.0 %copy-start.1 = (bf16[1536,128]{1,0:T(8,128)(2,1)S(1)}, bf16[1536,128]{1,0:T(8,128)(2,1)}, u32[]{:S(2)}) copy-start(bf16[1536,128]{1,0:T(8,128)(2,1)} %v_ref.1) | copy-start | bytes 1179652
  2.8 7.4 %collective-permute-start.2 = (f32[24,128]{1,0:T(8,128)S(1)}, f32[24,128]{1,0:T(8,128)S(1)}, u32[]{:S(2)}, u32[]{:S(2)}) collective-permute-start(f32[24,128]{1,0:T(8,128)S(1)} %squares.1.s0_ref), channel_id=1, source_target_pairs={{0,3},{1,0},{2,1},{3,2},{4,7},{5,4},{6,5},{7,6},{8,11},{9,8},{10,9... | collective-permute-start | bytes 36872 | tf_op jit(solution)/shard_map/ppermute | solution.py:505
  6.5 4.1 %collective-permute-start.1 = (f32[24,128]{1,0:T(8,128)S(1)}, f32[24,128]{1,0:T(8,128)S(1)}, u32[]{:S(2)}, u32[]{:S(2)}) collective-permute-start(f32[24,128]{1,0:T(8,128)S(1)} %squares.1.s0_ref), channel_id=1, source_target_pairs={{0,2},{1,3},{2,0},{3,1},{4,6},{5,7},{6,4},{7,5},{8,10},{9,11},{10,... | collective-permute-start | bytes 36872 | tf_op jit(solution)/shard_map/ppermute | solution.py:505
  6.8 3.8 %collective-permute-start = (f32[24,128]{1,0:T(8,128)S(1)}, f32[24,128]{1,0:T(8,128)S(1)}, u32[]{:S(2)}, u32[]{:S(2)}) collective-permute-start(f32[24,128]{1,0:T(8,128)S(1)} %squares.1.s0_ref), channel_id=1, source_target_pairs={{0,1},{1,2},{2,3},{3,0},{4,5},{5,6},{6,7},{7,4},{8,9},{9,10},{10,1... | collective-permute-start | bytes 36872 | tf_op jit(solution)/shard_map/ppermute | solution.py:505
  21.3 17.8 %collective-permute-start.5 = (f32[24,128]{1,0:T(8,128)S(1)}, f32[24,128]{1,0:T(8,128)S(1)}, u32[]{:S(2)}, u32[]{:S(2)}) collective-permute-start(f32[24,128]{1,0:T(8,128)S(1)} %get-tuple-element.22.s0_ref), channel_id=1, source_target_pairs={{0,3},{1,0},{2,1},{3,2},{4,7},{5,4},{6,5},{7,6},{8,11},{9,8},{10,9... | collective-permute-start | bytes 36872 | tf_op jit(solution)/shard_map/ppermute | solution.py:505
  23.0 16.1 %collective-permute-start.4 = (f32[24,128]{1,0:T(8,128)S(1)}, f32[24,128]{1,0:T(8,128)S(1)}, u32[]{:S(2)}, u32[]{:S(2)}) collective-permute-start(f32[24,128]{1,0:T(8,128)S(1)} %get-tuple-element.22.s0_ref), channel_id=1, source_target_pairs={{0,2},{1,3},{2,0},{3,1},{4,6},{5,7},{6,4},{7,5},{8,10},{9,11},{10,... | collective-permute-start | bytes 36872 | tf_op jit(solution)/shard_map/ppermute | solution.py:505
  24.4 14.7 %collective-permute-start.3 = (f32[24,128]{1,0:T(8,128)S(1)}, f32[24,128]{1,0:T(8,128)S(1)}, u32[]{:S(2)}, u32[]{:S(2)}) collective-permute-start(f32[24,128]{1,0:T(8,128)S(1)} %get-tuple-element.22.s0_ref), channel_id=1, source_target_pairs={{0,1},{1,2},{2,3},{3,0},{4,5},{5,6},{6,7},{7,4},{8,9},{9,10},{10,1... | collective-permute-start | bytes 36872 | tf_op jit(solution)/shard_map/ppermute | solution.py:505
  24.4 24.8 %all-to-all-start = ((f32[64,2,128]{2,1,0:T(2,128)}), f32[64,2,128]{2,1,0:T(2,128)S(1)}, u32[]{:S(2)}, u32[]{:S(2)}) async-start(f32[64,2,128]{2,1,0:T(2,128)} %get-tuple-element.26), calls=%async_computation | async-start | bytes 131072 | tf_op jit(solution)/shard_map/all_to_all | solution.py:565
